TPU v7x, 256 devices: a whole 4x4x8 slice. The times are simulated.
256 devices in a mesh: section: 2 (over core), seq: 32 (over y, z), mp: 4 (over x).
Axes of the slice: x: 4, y: 4, z: 8, core: 2. Of those that a mesh axis runs over, the one named last changes fastest.
Arguments:
- queries: bfloat16 [8192, 3072], P(('section', 'seq'), 'mp'), may hold values from -5 to 5
- keys: bfloat16 [8192, 3072], P(('section', 'seq'), 'mp'), may hold values from -5 to 5
- values: bfloat16 [8192, 3072], P(('section', 'seq'), 'mp'), may hold values from -6 to 6
- residual: bfloat16 [8192, 3072], P(('section', 'seq'), 'mp'), may hold values from -6 to 6
- segment_ids: int32 [2, 4096], P('section'), may hold values from 0 to 15, never falling along the last dimension, each value on 1 to 2048 neighbouring positions
- enc_counts: int32 [2, 32], P('section'), may hold values from 1 to 256, 4096 in all within a row
- enc_hidden: bfloat16 [16384, 4096], P(('section', 'seq'), 'mp'), may hold values from -6 to 6
- enc_down: bfloat16 [4096, 1536], P('mp'), may hold values from -0.09375 to 0.09375
- enc_resid: bfloat16 [16384, 1536], P(('section', 'seq'), 'mp'), may hold values from -6 to 6
- layer_scale: float32 [1536], replicated, may hold values from 0.2 to 2
- norm_gain: float32 [1536], replicated, may hold values from 0.25 to 1.75
- norm_bias: float32 [1536], replicated, may hold values from -3 to 3
- proj_in: bfloat16 [3072, 2048], P('mp'), may hold values from -0.109375 to 0.109375
- proj_out: bfloat16 [2048, 1536], P(None, 'mp'), may hold values from -0.125 to 0.125
- align_weight: float32 [8192], P(('section', 'seq')), may hold values from 2 to 20
Outputs:
- aligned: float32 [8192], P(('section', 'seq'))
- grad_in_t: float32 [2048, 3072], P(('section', 'seq'), 'mp')
- grad_out: float32 [2048, 1536], P(('section', 'seq'), 'mp')
Inputs may be any that keep to these rules, and one draw needn't show every extreme that they name: `enc_counts`: in each micro-batch the counts sum to 4096; some device holds exactly 256 valid rows. Rows of an encoder device beyond its count are padding. `segment_ids`: each image covers consecutive positions, ids never fall along a micro-batch.
All inputs are finite; a program needn't handle non-finite values.
Results may differ from a plain program's by a relative error of at most 0.025.
Values may be sent and summed in bfloat16 or wider, within the bound.
A program may use at most 128 MiB of HBM per device.

v0:
```python
import math

import jax
import jax.numpy as jnp
from jax import lax
from jax.sharding import PartitionSpec as P

HD = 128
ENC_D = 1536


def pack_rows(block, shift_amount, seq_count):
    capacity, columns = block.shape
    grid = block.reshape(capacity // seq_count, seq_count, columns).transpose(1, 0, 2)
    return jnp.roll(grid, shift_amount, axis=0)


def unpack_rows(received, offsets, seq_index, row_count):
    seq_count, slot_count, columns = received.shape
    flat_rows = received.reshape(seq_count * slot_count, columns)
    wanted = jnp.arange(row_count, dtype=jnp.int32) * seq_count + seq_index
    source = jnp.sum((offsets[None, :] <= wanted[:, None]).astype(jnp.int32), axis=1) - 1
    slot_index = (wanted - offsets[source]) // seq_count
    return flat_rows[source * slot_count + slot_index]


def body(
    queries,
    keys,
    values,
    residual,
    segment_ids,
    enc_counts,
    enc_hidden,
    enc_down,
    enc_resid,
    layer_scale,
    norm_gain,
    norm_bias,
    proj_in,
    proj_out,
    align_weight,
):
    seq_count = lax.axis_size("seq")
    seq_index = lax.axis_index("seq")
    mp_index = lax.axis_index("mp")
    row_count = queries.shape[0]
    local_width = queries.shape[1]
    head_count = local_width // HD
    capacity = enc_hidden.shape[0]
    channels = enc_resid.shape[1]
    seg_order = segment_ids[0].reshape(row_count, seq_count).T.reshape(-1)
    query_segs = lax.dynamic_slice_in_dim(seg_order, seq_index * row_count, row_count)
    query_heads = queries.reshape(row_count, head_count, HD)
    score_scale = HD ** (-0.5)
    start_state = (
        jnp.full((head_count, row_count), -1e30, jnp.float32),
        jnp.zeros((head_count, row_count), jnp.float32),
        jnp.zeros((head_count, row_count, HD), jnp.float32),
    )
    key_piece = lax.all_gather(keys, "seq", axis=0, tiled=True)
    value_piece = lax.all_gather(values, "seq", axis=0, tiled=True)
    key_rows = key_piece.shape[0]
    block_rows = math.gcd(key_rows, 1024)
    block_count = key_rows // block_rows
    key_blocks = key_piece.reshape(block_count, block_rows, head_count, HD)
    value_blocks = value_piece.reshape(block_count, block_rows, head_count, HD)

    def one_block(state, items):
        best, total, accum = state
        key_block, value_block, block_id = items
        key_segs = lax.dynamic_slice_in_dim(seg_order, block_id * block_rows, block_rows)
        scores = (
            jnp.einsum("qhd,khd->hqk", query_heads, key_block, preferred_element_type=jnp.float32)
            * score_scale
        )
        allowed = (query_segs[:, None] == key_segs[None, :])[None]
        scores = jnp.where(allowed, scores, -1e30)
        new_best = jnp.maximum(best, jnp.max(scores, axis=-1))
        weights = jnp.where(allowed, jnp.exp(scores - new_best[..., None]), 0.0)
        factor = jnp.exp(best - new_best)
        total = total * factor + jnp.sum(weights, axis=-1)
        mixed = jnp.einsum(
            "hqk,khd->hqd",
            weights.astype(jnp.bfloat16),
            value_block,
            preferred_element_type=jnp.float32,
        )
        accum = accum * factor[..., None] + mixed
        return ((new_best, total, accum), None)

    result, unused = lax.scan(
        one_block, start_state, (key_blocks, value_blocks, jnp.arange(block_count, dtype=jnp.int32))
    )
    best, total, accum = result
    attn = (
        (accum / total[..., None])
        .transpose(1, 0, 2)
        .reshape(row_count, local_width)
        .astype(jnp.bfloat16)
    )
    attn = lax.optimization_barrier(attn)
    hidden = (residual.astype(jnp.float32) + attn.astype(jnp.float32)).astype(jnp.bfloat16)
    counts = enc_counts[0]
    offsets = jnp.cumsum(counts) - counts
    my_offset = offsets[seq_index]
    my_count = counts[seq_index]
    shift_amount = my_offset % seq_count
    gain_part = lax.dynamic_slice_in_dim(norm_gain, mp_index * channels, channels)
    bias_part = lax.dynamic_slice_in_dim(norm_bias, mp_index * channels, channels)
    keep_rows = (jnp.arange(capacity) < my_count)[:, None]
    partial_value = jnp.dot(enc_hidden, enc_down, preferred_element_type=jnp.float32)
    placed = lax.dynamic_update_slice(
        jnp.zeros(partial_value.shape, jnp.float32),
        enc_resid.astype(jnp.float32),
        (0, mp_index * channels),
    )
    term = layer_scale[None, :] * partial_value + placed
    share = lax.psum_scatter(
        term.astype(jnp.bfloat16), "mp", scatter_dimension=1, tiled=True
    ).astype(jnp.float32)
    sums, squares = lax.psum((jnp.sum(share, axis=1), jnp.sum(share * share, axis=1)), "mp")
    mean = sums / ENC_D
    meansq = squares / ENC_D
    variance = meansq - mean * mean
    features = (
        (share - mean[:, None]) * lax.rsqrt(variance + 1e-06)[:, None] * gain_part[None, :]
        + bias_part[None, :]
    ).astype(jnp.bfloat16)
    features = jnp.where(keep_rows, features, 0)
    moved = lax.all_to_all(
        pack_rows(features, shift_amount, seq_count), "seq", split_axis=0, concat_axis=0, tiled=True
    )
    target = unpack_rows(moved, offsets, seq_index, row_count)
    first = lax.psum(
        jnp.dot(hidden, proj_in, preferred_element_type=jnp.float32).astype(jnp.bfloat16), "mp"
    ).astype(jnp.float32)
    act = jax.nn.silu(first).astype(jnp.bfloat16)
    second = jnp.dot(act, proj_out, preferred_element_type=jnp.float32)
    target_f = target.astype(jnp.float32)
    inner, square_z, square_f = lax.psum(
        (
            jnp.sum(second * target_f, axis=1),
            jnp.sum(second * second, axis=1),
            jnp.sum(target_f * target_f, axis=1),
        ),
        "mp",
    )
    norm_z = jnp.sqrt(square_z + 1e-06)
    norm_f = jnp.sqrt(square_f + 1e-06)
    aligned = inner / (norm_z * norm_f)
    back = (
        -align_weight[:, None]
        * (target_f / (norm_z * norm_f)[:, None] - (aligned / (norm_z * norm_z))[:, None] * second)
    ).astype(jnp.bfloat16)
    upstream = lax.psum(
        lax.dot_general(
            back, proj_out, (((1,), (1,)), ((), ())), preferred_element_type=jnp.float32
        ).astype(jnp.bfloat16),
        "mp",
    ).astype(jnp.float32)
    sig = jax.nn.sigmoid(first)
    dfirst = (upstream * sig * (1.0 + first * (1.0 - sig))).astype(jnp.bfloat16)
    grad_out = lax.psum_scatter(
        lax.dot_general(act, back, (((0,), (0,)), ((), ())), preferred_element_type=jnp.float32),
        ("section", "seq"),
        scatter_dimension=0,
        tiled=True,
    )
    grad_in_t = lax.psum_scatter(
        lax.dot_general(
            dfirst, hidden, (((0,), (0,)), ((), ())), preferred_element_type=jnp.float32
        ),
        ("section", "seq"),
        scatter_dimension=0,
        tiled=True,
    )
    return (aligned, grad_in_t, grad_out)


def solution(mesh):
    return jax.shard_map(
        body,
        mesh=mesh,
        in_specs=(
            P(("section", "seq"), "mp"),
            P(("section", "seq"), "mp"),
            P(("section", "seq"), "mp"),
            P(("section", "seq"), "mp"),
            P("section", None),
            P("section", None),
            P(("section", "seq"), "mp"),
            P("mp", None),
            P(("section", "seq"), "mp"),
            P(),
            P(),
            P(),
            P("mp", None),
            P(None, "mp"),
            P(("section", "seq")),
        ),
        out_specs=(P(("section", "seq")), P(("section", "seq"), "mp"), P(("section", "seq"), "mp")),
        check_vma=False,
    )
```

profile of v0, /device:TPU:1, one launch (start us, length us, event | category | flops | bytes accessed | tf_op | source)
XLA Modules:
  0.0 660.3 jit_solution(12729896419776052752)
XLA Ops:
  8.1 1.8 copy-done
  9.9 2.0 convolution_multiply_fusion
  12.2 1.2 copy.62
  18.0 0.8 dynamic_slice.35
  18.8 0.8 dynamic_slice.36
  21.1 0.8 copy.52
  22.9 18.3 %reduce-scatter.10.cloned.1.call-done = bf16[384,256]{1,0:T(8,128)(2,1)} async-done(((bf16[1536,256]{1,0:T(8,128)(2,1)}), bf16[384,256]{1,0:T(8,128)(2,1)}) %reduce-scatter.10.cloned.1.call-update) | async-done | bytes 196624
  41.2 1.1 copy.63
  42.5 6.6 all-reduce.1
  49.2 0.7 copy.65
  50.0 58.1 %all-gather.3.cloned.1.call-done = bf16[4096,768]{1,0:T(8,128)(2,1)} async-done(((bf16[128,768]{1,0:T(8,128)(2,1)}), bf16[4096,768]{1,0:T(8,128)(2,1)}) %all-gather.3.cloned.1.call-update) | async-done | bytes 6291472 | tf_op jit(solution)/shard_map/all_gather | solution.py:61
  108.0 13.7 %reshape.211 = bf16[4,1024,6,128]{3,2,1,0:T(8,128)(2,1)} reshape(bf16[4096,768]{1,0:T(8,128)(2,1)} %all-gather.3.cloned.1.call-done) | data formatting | bytes 12582912 | tf_op jit(solution)/shard_map/reshape | solution.py:66
  121.7 7.5 %copy.51 = bf16[4,1024,6,128]{3,1,2,0:T(8,128)(2,1)} copy(bf16[4,1024,6,128]{3,2,1,0:T(8,128)(2,1)} %reshape.211) | data formatting | bytes 12582912
  129.2 66.8 %all-gather.5.cloned.1.call-done = bf16[4096,768]{1,0:T(8,128)(2,1)} async-done(((bf16[128,768]{1,0:T(8,128)(2,1)}), bf16[4096,768]{1,0:T(8,128)(2,1)}) %all-gather.5.cloned.1.call-update) | async-done | bytes 6291472 | tf_op jit(solution)/shard_map/all_gather | solution.py:62
  196.0 13.7 %reshape.212 = bf16[4,1024,6,128]{3,2,1,0:T(8,128)(2,1)} reshape(bf16[4096,768]{1,0:T(8,128)(2,1)} %all-gather.5.cloned.1.call-done) | data formatting | bytes 12582912 | tf_op jit(solution)/shard_map/reshape | solution.py:67
  209.6 7.3 %copy.53 = bf16[4,1024,6,128]{3,1,2,0:T(8,128)(2,1)} copy(bf16[4,1024,6,128]{3,2,1,0:T(8,128)(2,1)} %reshape.212) | data formatting | bytes 12582912
  217.0 32.5 %while.15 = (s32[]{:T(128)}, f32[6,128]{1,0:T(8,128)S(1)}, f32[6,128]{1,0:T(8,128)S(1)}, f32[6,128,128]{2,1,0:T(8,128)}, s32[128]{0:T(128)S(1)}, /*index=5*/s32[...) while((s32[]{:T(128)}, f32[6,128]{1,0:T(8,128)S(1)}, ...), condition=%wide.region_3.4_spmd.clone, body=%wide.region_0.3_spmd.clone.sunk | while | flops 413306624 | bytes 17299208 | solution.py:92
  218.4 2.1 fusion.75
  220.5 0.8 fusion.76
  221.5 2.8 fusion.78
  224.3 0.7 copy-done.6
  226.6 2.1 fusion.75
  228.6 0.8 fusion.76
  229.6 2.8 fusion.78
  232.5 0.7 copy-done.6
  234.7 2.1 fusion.75
  236.8 0.8 fusion.76
  237.7 2.8 fusion.78
  240.6 0.7 copy-done.6
  242.8 2.1 fusion.75
  244.9 0.8 fusion.76
  245.8 2.8 fusion.78
  249.4 1.2 copy.54
  250.7 3.4 convolution_convert_fusion.1
  254.2 0.9 fusion.46
  255.1 5.6 all-to-all-start
  260.9 1.2 gather_fusion
  262.2 7.9 %all-to-all-done = bf16[32,8,384]{2,1,0:T(8,128)(2,1)S(1)} async-done(((bf16[32,8,384]{2,1,0:T(8,128)(2,1)}), bf16[32,8,384]{2,1,0:T(8,128)(2,1)S(1)}, u32[]{:S(2)}, u32[]{:S(2)}) %all-to-all-start) | async-done | bytes 196640 | tf_op jit(solution)/shard_map/all_to_all | solution.py:131
  270.1 0.9 gather_fusion.1
  271.0 27.3 %all-reduce.5.cloned.1.call-done = bf16[128,2048]{1,0:T(8,128)(2,1)} async-done(((bf16[128,2048]{1,0:T(8,128)(2,1)}), bf16[128,2048]{1,0:T(8,128)(2,1)}) %all-reduce.5.cloned.1.call-update) | async-done | bytes 524304 | tf_op jit(solution)/shard_map/psum | solution.py:135
  298.3 1.7 multiply_reduce_fusion
  300.0 7.9 %all-reduce = (f32[128]{0:T(128)S(1)}, f32[128]{0:T(128)S(1)}, f32[128]{0:T(128)S(1)}) all-reduce(f32[128]{0:T(128)S(1)} %get-tuple-element.122, f32[128]{0:T(128)S(1)} %get-tuple-element.125, f32[128]{0:T(128)S(1)} %get-tuple-element.121), channel_id=1, replica_groups=mesh['section'=2,'seq'=32,'mp'=4] {'mp'}, use_global_device_ids=true, to_apply=%region_13.14 | all-reduce | flops 384 | bytes 3072 | tf_op jit(solution)/shard_map/psum | solution.py:141
  307.9 1.5 convolution_convert_fusion
  309.4 2.4 fusion.53
  311.9 46.5 %all-reduce.7.cloned.1.call-done = bf16[128,2048]{1,0:T(8,128)(2,1)} async-done(((bf16[128,2048]{1,0:T(8,128)(2,1)}), bf16[128,2048]{1,0:T(8,128)(2,1)}) %all-reduce.7.cloned.1.call-update) | async-done | bytes 524304 | tf_op jit(solution)/shard_map/psum | solution.py:156
  358.4 5.1 fusion.33
  364.0 138.3 %reduce-scatter.8.cloned.1.call-done = f32[32,384]{1,0:T(8,128)} async-done(((f32[2048,384]{1,0:T(8,128)}), f32[32,384]{1,0:T(8,128)}) %reduce-scatter.8.cloned.1.call-update) | async-done | bytes 49168 | tf_op jit(solution)/shard_map/reduce_scatter | solution.py:164
  502.3 150.9 %reduce-scatter.6.cloned.1.call-done = f32[32,768]{1,0:T(8,128)} async-done(((f32[2048,768]{1,0:T(8,128)}), f32[32,768]{1,0:T(8,128)}) %reduce-scatter.6.cloned.1.call-update) | async-done | bytes 98320 | tf_op jit(solution)/shard_map/reduce_scatter | solution.py:170
  (106 shorter events, 11.5 us)
Async XLA Ops:
  8.0 1.9 copy-start
  8.0 3.9 copy-start.7
  8.0 33.2 %reduce-scatter.10.cloned.1.call-start = ((), (), s32[]{:S(2)}) async-start(), calls=%async_computation.10 | async-start | bytes 983040
  11.9 2.6 copy-start.11
  11.9 8.1 %copy-start.10 = (s32[1,4096]{1,0:T(1,128)S(1)}, s32[1,4096]{1,0:T(1,128)}, u32[]{:S(2)}) copy-start(s32[1,4096]{1,0:T(1,128)} %param.21) | copy-start | bytes 49156
  12.0 8.9 %copy-start.8 = (bf16[128,768]{1,0:T(8,128)(2,1)S(1)}, bf16[128,768]{1,0:T(8,128)(2,1)}, u32[]{:S(2)}) copy-start(bf16[128,768]{1,0:T(8,128)(2,1)} %param.17) | copy-start | bytes 589828
  12.1 9.8 %copy-start.9 = (bf16[128,768]{1,0:T(8,128)(2,1)S(1)}, bf16[128,768]{1,0:T(8,128)(2,1)}, u32[]{:S(2)}) copy-start(bf16[128,768]{1,0:T(8,128)(2,1)} %param.20) | copy-start | bytes 589828
  13.3 94.7 %all-gather.3.cloned.1.call-start = ((), (), s32[]{:S(2)}) async-start(), calls=%async_computation.4 | async-start | bytes 6488064 | tf_op jit(solution)/shard_map/all_gather | solution.py:61
  13.9 182.1 %all-gather.5.cloned.1.call-start = ((), (), s32[]{:S(2)}) async-start(), calls=%async_computation.5 | async-start | bytes 6488064 | tf_op jit(solution)/shard_map/all_gather | solution.py:62
  14.5 283.8 %all-reduce.5.cloned.1.call-start = ((), (), s32[]{:S(2)}) async-start(), calls=%async_computation.6 | async-start | bytes 1048576 | tf_op jit(solution)/shard_map/psum | solution.py:135
  220.5 1.0 copy-start.5
  224.3 0.8 copy-start.6
  228.6 1.0 copy-start.5
  232.5 0.8 copy-start.6
  236.7 1.0 copy-start.5
  240.6 0.8 copy-start.6
  244.9 1.0 copy-start.5
  248.7 0.8 copy-start.6
  249.4 4.7 copy-start.4
  250.6 11.5 %copy-start.12 = (f32[128]{0:T(128)S(1)}, f32[128]{0:T(128)}, u32[]{:S(2)}) copy-start(f32[128]{0:T(128)} %param.31) | copy-start | bytes 1540
  250.7 47.6 %copy-start.3 = (bf16[2048,384]{1,0:T(8,128)(2,1)S(1)}, bf16[2048,384]{1,0:T(8,128)(2,1)}, u32[]{:S(2)}) copy-start(bf16[2048,384]{1,0:T(8,128)(2,1)} %param.30) | copy-start | bytes 4718596
  255.1 15.0 %all-to-all-start = ((bf16[32,8,384]{2,1,0:T(8,128)(2,1)}), bf16[32,8,384]{2,1,0:T(8,128)(2,1)S(1)}, u32[]{:S(2)}, u32[]{:S(2)}) async-start(bf16[32,8,384]{2,1,0:T(8,128)(2,1)} %fusion.46), calls=%async_computation | async-start | bytes 393216 | tf_op jit(solution)/shard_map/all_to_all | solution.py:131
  260.7 97.7 %all-reduce.7.cloned.1.call-start = ((), (), s32[]{:S(2)}) async-start(), calls=%async_computation.7 | async-start | bytes 1048576 | tf_op jit(solution)/shard_map/psum | solution.py:156
  298.3 11.2 %copy-start.2 = (bf16[128,2048]{1,0:T(8,128)(2,1)S(1)}, bf16[128,2048]{1,0:T(8,128)(2,1)}, u32[]{:S(2)}) copy-start(bf16[128,2048]{1,0:T(8,128)(2,1)} %all-reduce.5.cloned.1.call-done) | copy-start | bytes 1572868
  309.4 192.9 %reduce-scatter.8.cloned.1.call-start = ((), (), s32[]{:S(2)}) async-start(), calls=%async_computation.9 | async-start | bytes 3194880 | tf_op jit(solution)/shard_map/reduce_scatter | solution.py:164
  311.8 341.4 %reduce-scatter.6.cloned.1.call-start = ((), (), s32[]{:S(2)}) async-start(), calls=%async_computation.8 | async-start | bytes 6389760 | tf_op jit(solution)/shard_map/reduce_scatter | solution.py:170
  363.4 289.8 %copy-start.1 = (bf16[1024,1536]{1,0:T(8,128)(2,1)S(1)}, bf16[1024,1536]{1,0:T(8,128)(2,1)}, u32[]{:S(2)}) copy-start(bf16[1024,1536]{1,0:T(8,128)(2,1)} %param.24) | copy-start | bytes 9437188
Sparse Core Ops, SparseCore 0:
  13.5 27.7 reduce-scatter.9
  254.3 43.9 all-reduce.4
  309.5 48.8 all-reduce.6
  362.9 139.3 reduce-scatter.7
  506.9 146.2 reduce-scatter.5
Sparse Core Ops, SparseCore 1:
  16.4 91.6 all-gather.2
  110.5 85.4 all-gather.4
where the time goes:
time: 666 us; the launch traced here: 660 us
  waiting for transfers between devices  515 us (77%)
  local copies, waits for them, and re-layouts  61.1 us (9%)
  matrix products  35.6 us (5%)
  between operations  17.5 us (3%)
  blocking collectives  14.4 us (2%)
  other arithmetic  7.58 us (1%)
    reduce_scatter x1, waiting for transfers between devices, body(): lax.psum_scatter(lax.dot_general(dfirst, hidden, (((0,), (0,)), ((), ()))...  151 us
    reduce_scatter x1, waiting for transfers between devices, body(): lax.psum_scatter(lax.dot_general(act, back, (((0,), (0,)), ((), ())), pre...  138 us
    all_gather x1, waiting for transfers between devices, body(): value_piece = lax.all_gather(values, 'seq', axis=0, tiled=True)  66.8 us
    all_gather x1, waiting for transfers between devices, body(): key_piece = lax.all_gather(keys, 'seq', axis=0, tiled=True)  58.1 us
    psum x1, waiting for transfers between devices, body(): lax.psum(lax.dot_general(back, proj_out, (((1,), (1,)), ((), ())), prefer...  46.5 us
    psum x1, waiting for transfers between devices, body(): lax.psum(jnp.dot(hidden, proj_in, preferred_element_type=jnp.float32).ast...  27.3 us
    unnamed x30, local copies, waits for them, and re-layouts  20.6 us
    unnamed x8, waiting for transfers between devices  19.4 us
  transfers between devices with their start and end apart: 8, of which 8 were waited for; matrix products, arithmetic and copies ran while one was open for 6% of the time, Pallas kernels for 0%

commit v1 on v0

v1 whole, which is shorter than its diff:
```python
import math

import jax
import jax.numpy as jnp
from jax import lax
from jax.experimental import pallas as pl
from jax.experimental.pallas import tpu as pltpu
from jax.sharding import PartitionSpec as P

MESH = pl.DeviceIdType.MESH
F32, BF16, I32 = jnp.float32, jnp.bfloat16, jnp.int32
HD = 128
ENC_D = 1536
NX, NY, NZ = 4, 4, 8
NSEQ = NY * NZ
ROWS = 128
CAP = 256
WIDTH = 768
HEADS = 6
HALF = 384
CH = 384
FF = 1024
PROJ = 2048
PART = 512
SAME = 8192.0
EXP_SCALE = math.log2(math.e) * HD ** (-0.5)


def rcopy(src, dst, send, recv, dev):
    return pltpu.make_async_remote_copy(
        src_ref=src, dst_ref=dst, send_sem=send, recv_sem=recv, device_id=dev, device_id_type=MESH
    )


def iota(shape, dim):
    return lax.broadcasted_iota(I32, shape, dim)


def dot(a, b, ca=1, cb=0):
    return lax.dot_general(a, b, (((ca,), (cb,)), ((), ())), preferred_element_type=F32)


def kernel(
    q_hbm, k_hbm, v_hbm, res_hbm, seg_ref, cnt_ref, eh_hbm, ed_hbm, er_hbm, ls_ref, gain_ref, bias_ref,
    pin_hbm, pout_hbm, aw_ref,
    al_ref, gi_ref, go_ref,
    qbuf, kbuf, vbuf, vt, ko, resv, ehv, edv, erv, pin, pout,
    opart, stats, oin, sin,
    esend, erecv, share, estat, estat_in, packed, arecv, target,
    hidden, fsend, frecv, first, actbuf, second, sstat, sstat_in, back, dbuf, segrow,
    go_x, go_xr, go_h, go_yr, go_z, go_zr,
    gi_x, gi_xr, gi_h, gi_yr, gi_z, gi_zr,
    lsem, q_s, q_r, kv_s, kv_r, o_s, o_r, os_s, os_r, x_s, x_r, a_s, a_r,
    gx_s, gx_r, gy_s, gy_r, gz_s, gz_r,
):
    sec = lax.axis_index("section")
    seq = lax.axis_index("seq")
    x = lax.axis_index("mp")
    y = seq // NZ
    z = lax.rem(seq, NZ)
    zp = {"seq": y * NZ + lax.rem(z + 1, NZ)}
    zm = {"seq": y * NZ + lax.rem(z + NZ - 1, NZ)}
    yp = {"seq": lax.rem(y + 1, NY) * NZ + z}
    ym = {"seq": lax.rem(y + NY - 1, NY) * NZ + z}
    pending = []

    def go(copy):
        copy.start()
        pending.append(copy)
        return copy

    local = []
    for n, (src, dst) in enumerate((
        (q_hbm, qbuf.at[0]), (k_hbm, kbuf.at[0]), (v_hbm, vbuf.at[0]), (eh_hbm, ehv), (ed_hbm, edv),
        (er_hbm, erv), (res_hbm, resv), (pin_hbm, pin), (pout_hbm, pout),
    )):
        copy = pltpu.make_async_copy(src, dst, lsem.at[n])
        copy.start()
        local.append(copy)

    barrier = pltpu.get_barrier_semaphore()

    def greet(i, c):
        pl.semaphore_signal(barrier, inc=1, device_id={"seq": lax.rem(seq + i, NSEQ)}, device_id_type=MESH)
        return c

    lax.fori_loop(1, NSEQ, greet, 0)
    for r in range(1, NX):
        pl.semaphore_signal(barrier, inc=1, device_id={"mp": lax.rem(x + r, NX)}, device_id_type=MESH)
    pl.semaphore_signal(barrier, inc=1, device_id={"section": 1 - sec}, device_id_type=MESH)
    pl.semaphore_wait(barrier, NSEQ - 1 + NX - 1 + 1)

    def q_copy(d, t):
        slot = (8 - t) % 8 if d == 0 else t
        to = 7 - t if d == 0 else t + 1
        src, dst = qbuf.at[slot], qbuf.at[to]
        if t == 3:
            cols = pl.ds(d * HALF, HALF)
            src, dst = qbuf.at[slot, :, cols], qbuf.at[to, :, cols]
        return rcopy(src, dst, q_s.at[d, t], q_r.at[d, t], zp if d == 0 else zm)

    def kv_copy(n):
        src, dst, dev = (
            (kbuf.at[0], kbuf.at[3], yp), (kbuf.at[0], kbuf.at[1], ym),
            (vbuf.at[0], vbuf.at[3], yp), (vbuf.at[0], vbuf.at[1], ym),
            (kbuf.at[3], kbuf.at[2], yp), (vbuf.at[1], vbuf.at[2], ym),
        )[n]
        return rcopy(src, dst, kv_s.at[n], kv_r.at[n], dev)

    q_copies = [[q_copy(d, t) for t in range(4)] for d in range(2)]
    kv_copies = [kv_copy(n) for n in range(6)]
    local[0].wait()
    go(q_copies[0][0])
    go(q_copies[1][0])
    local[1].wait()
    go(kv_copies[0])
    go(kv_copies[1])
    local[2].wait()
    go(kv_copies[2])
    go(kv_copies[3])

    def x_copies(phase, src_of, dst_of):
        return {
            r: rcopy(src_of(r), dst_of(NX - r), x_s.at[phase, r - 1], x_r.at[phase, NX - r - 1],
                     {"mp": lax.rem(x + r, NX)})
            for r in (1, 2, 3)
        }

    local[3].wait()
    local[4].wait()
    enc_copies = x_copies(0, lambda r: esend.at[r], lambda r: erecv.at[r])
    for r in (2, 1, 3, 0):
        cols = pl.ds(pl.multiple_of(lax.rem(x + r, NX) * CH, CH), CH)
        esend[r] = dot(ehv[...], edv[:, cols]).astype(BF16)
        if r:
            go(enc_copies[r])

    ids = iota((16, NSEQ * ROWS), 0)
    seg = seg_ref[...]
    below = jnp.sum(jnp.where(seg < ids, 1.0, 0.0), axis=1, keepdims=True)
    upto = jnp.sum(jnp.where(seg <= ids, 1.0, 0.0), axis=1, keepdims=True)
    lane = iota((16, HD), 1)
    tail = jnp.full((HD - 16, HD), 1e9, F32)
    segrow[0] = jnp.concatenate([jnp.broadcast_to(below, lane.shape), tail], axis=0).T
    segrow[1] = jnp.concatenate([jnp.broadcast_to(upto, lane.shape), tail], axis=0).T

    def image_columns(device):
        place = (iota((ROWS, HD), 0) * NSEQ + device).astype(F32)
        return (place >= segrow[0]) & (place < segrow[1])

    for r in range(NY):
        device = lax.rem(y + r, NY) * NZ + z
        ko[r] = jnp.where(image_columns(device), SAME, 0.0).astype(BF16)

    def forward_q(t):
        for d in range(2):
            q_copies[d][t].wait_recv()
            if t < 3:
                go(q_copies[d][t + 1])

    forward_q(0)
    kv_copies[0].wait_recv()
    go(kv_copies[4])
    kv_copies[1].wait_recv()

    local[5].wait()
    own = pl.ds(pl.multiple_of(x * CH, CH), CH)
    for r in (1, 2, 3):
        enc_copies[NX - r].wait_recv()
    enc = esend[0].astype(F32)
    for r in (1, 2, 3):
        enc = enc + erecv[r].astype(F32)
    enc = erv[...].astype(F32) + ls_ref[:, own] * enc
    share[...] = enc
    lane = iota((CAP, HD), 1)
    total = jnp.sum(enc, axis=1, keepdims=True)
    square = jnp.sum(enc * enc, axis=1, keepdims=True)
    packed_stat = jnp.where(lane == 0, total, jnp.where(lane == 1, square, 0.0))
    for b in range(2):
        estat[:, b * HD:(b + 1) * HD] = packed_stat[b * HD:(b + 1) * HD].T[0:8]
    stat_copies = x_copies(1, lambda r: estat, lambda r: estat_in.at[r])
    for r in (2, 1, 3):
        go(stat_copies[r])

    kv_copies[2].wait_recv()
    kv_copies[3].wait_recv()
    go(kv_copies[5])
    forward_q(1)

    for r in (1, 2, 3):
        stat_copies[NX - r].wait_recv()
    both = estat[...]
    for r in (1, 2, 3):
        both = both + estat_in[r]
    mean = both[0:1] * (1.0 / ENC_D)
    scale = lax.rsqrt(both[1:2] * (1.0 / ENC_D) - mean * mean + 1e-6)
    pad = jnp.zeros((HD - 8, HD), F32)
    row8 = iota((8, HD), 0)
    gain = gain_ref[:, own]
    bias = bias_ref[:, own]
    parts = []
    for b in range(2):
        cut = slice(b * HD, (b + 1) * HD)
        rows = jnp.where(row8 == 0, mean[:, cut], jnp.where(row8 == 1, scale[:, cut], 0.0))
        cols = jnp.concatenate([rows, pad], axis=0).T
        parts.append((((share[cut] - cols[:, 0:1]) * cols[:, 1:2]) * gain + bias).astype(BF16))
    feature = jnp.concatenate(parts, axis=0)
    counts = cnt_ref[...].astype(F32)
    before = jnp.sum(jnp.where(iota((1, NSEQ), 1) < seq, counts, 0.0), axis=1, keepdims=True).astype(I32)
    row = iota((CAP, CAP), 0)
    wanted = (row & 7) * NSEQ + (((row >> 3) - before) & (NSEQ - 1))
    permutation = jnp.where(iota((CAP, CAP), 1) == wanted, 1.0, 0.0).astype(BF16)
    packed[...] = dot(permutation, feature).reshape(NSEQ, 8, CH)

    def row_copy(peer, mine):
        return rcopy(packed.at[peer], arecv.at[mine], a_s.at[peer], a_r.at[mine], {"seq": peer})

    def send_rows(i, c):
        row_copy(lax.rem(seq + i, NSEQ), seq).start()
        return c

    lax.fori_loop(1, NSEQ, send_rows, 0)
    arecv[pl.ds(seq, 1)] = packed[pl.ds(seq, 1)]

    for n in (4, 5):
        kv_copies[n].wait_recv()
    for r in range(NY):
        vt[:, r * ROWS:(r + 1) * ROWS] = vbuf[r].T
    keys_image = ko[...].reshape(NY * ROWS, HD)

    def attend(r):
        device = y * NZ + lax.rem(z + r, NZ)
        image = jnp.where(image_columns(device), 1.0, 0.0).astype(BF16)
        for h in range(HEADS):
            cols = slice(h * HD, (h + 1) * HD)
            keys = jnp.concatenate([kbuf[:, :, cols].reshape(NY * ROWS, HD), keys_image], axis=1)
            scores = dot(keys, jnp.concatenate([qbuf[r, :, cols], image], axis=1), 1, 1)
            best = jnp.max(scores, axis=0, keepdims=True)
            prob = jnp.exp2((scores - best) * EXP_SCALE)
            half, i = h // 3, h % 3
            stats[r, half, i:i + 1] = best * EXP_SCALE
            stats[r, half, 3 + i:4 + i] = jnp.sum(prob, axis=0, keepdims=True)
            opart[r, half, i * HD:(i + 1) * HD] = dot(vt[cols], prob.astype(BF16)).astype(BF16)

    def o_copy(d, t):
        r = 4 - t if d == 0 else 4 + t
        dev = zp if d == 0 else zm
        src, dst, ssrc, sdst = opart.at[r], oin.at[d, t], stats.at[r], sin.at[d, t]
        if t == 0:
            src, dst, ssrc, sdst = src.at[d], dst.at[d], ssrc.at[d], sdst.at[d]
        return (rcopy(src, dst, o_s.at[d, t], o_r.at[d, t], dev),
                rcopy(ssrc, sdst, os_s.at[d, t], os_r.at[d, t], dev))

    o_copies = [[o_copy(d, t) for t in range(4)] for d in range(2)]

    def attend_some(i, c):
        attend(4 + (2 - i // 2) * (1 - 2 * lax.rem(i, 2)))
        return c

    lax.fori_loop(0, 2, attend_some, 0)
    forward_q(2)
    lax.fori_loop(2, 4, attend_some, 0)
    forward_q(3)
    lax.fori_loop(4, 5, attend_some, 0)
    for d in range(2):
        for copy in o_copies[d][0]:
            go(copy)

    def merge(r, d, t, half):
        mine, other = stats[r, half], sin[d, t, half]
        for i in range(3):
            m0, m1 = mine[i:i + 1], other[i:i + 1]
            best = jnp.maximum(m0, m1)
            f0, f1 = jnp.exp2(m0 - best), jnp.exp2(m1 - best)
            rows = slice(i * HD, (i + 1) * HD)
            mixed = opart[r, half, rows].astype(F32) * f0 + oin[d, t, half, rows].astype(F32) * f1
            opart[r, half, rows] = mixed.astype(BF16)
            stats[r, half, i:i + 1] = best
            stats[r, half, 3 + i:4 + i] = mine[3 + i:4 + i] * f0 + other[3 + i:4 + i] * f1

    for t in (1, 2, 3):
        if t > 1:
            def attend_rest(i, c):
                attend(lax.rem(7 + 2 * i, 8) if t == 2 else 0 * i)
                return c
            lax.fori_loop(0, 2 if t == 2 else 1, attend_rest, 0)
        for d in range(2):
            for copy in o_copies[d][t - 1]:
                copy.wait_recv()
            for half in range(2):
                if t > 1 or half == d:
                    merge(4 - t if d == 0 else 4 + t, d, t - 1, half)
            for copy in o_copies[d][t]:
                go(copy)
    for d in range(2):
        for copy in o_copies[d][3]:
            copy.wait_recv()
        for half in range(2):
            merge(0, d, 3, half)
    local[6].wait()
    for h in range(HEADS):
        half, i = h // 3, h % 3
        cols = slice(h * HD, (h + 1) * HD)
        attn = opart[0, half, i * HD:(i + 1) * HD].astype(F32) / stats[0, half, 3 + i:4 + i]
        attn = attn.T.astype(BF16).astype(F32)
        hidden[:, cols] = (resv[:, cols].astype(F32) + attn).astype(BF16)

    local[7].wait()
    f_copies = x_copies(2, lambda r: fsend.at[0, r], lambda r: frecv.at[0, r])
    for r in (2, 1, 3, 0):
        cols = pl.ds(pl.multiple_of(lax.rem(x + r, NX) * PART, PART), PART)
        fsend[0, r] = dot(hidden[...], pin[:, cols]).astype(BF16)
        if r:
            go(f_copies[r])

    e_of = iota((NSEQ, CAP), 1) >> 3
    device = iota((NSEQ, CAP), 0)
    counts8 = jnp.broadcast_to(counts, (8, NSEQ)).astype(BF16)
    start = dot(counts8, jnp.where(device < e_of, 1.0, 0.0).astype(BF16))[0:1]
    count = dot(counts8, jnp.where(device == e_of, 1.0, 0.0).astype(BF16))[0:1]
    low = start + ((iota((1, CAP), 1) & 7) * NSEQ).astype(F32)
    high = jnp.minimum(low + float(NSEQ), start + count)
    place = (iota((ROWS, CAP), 0) * NSEQ + seq).astype(F32)
    chosen = jnp.where((place >= low) & (place < high), 1.0, 0.0).astype(BF16)

    def take_rows(i, c):
        peer = lax.rem(seq + i, NSEQ)
        row_copy(seq, peer).wait_recv()
        return c

    lax.fori_loop(1, NSEQ, take_rows, 0)
    target[...] = dot(chosen, arecv[...].reshape(CAP, CH).astype(BF16))
    tf = target[...]

    def x_sum(phase, copies):
        for r in (1, 2, 3):
            copies[NX - r].wait_recv()
        value = fsend[phase, 0].astype(F32)
        for r in (1, 2, 3):
            value = value + frecv[phase, r].astype(F32)
        return value

    value = x_sum(0, f_copies)
    first[...] = value
    actbuf[0] = (value * jax.nn.sigmoid(value)).astype(BF16)
    act_copies = x_copies(3, lambda r: actbuf.at[0], lambda r: actbuf.at[r])
    for r in (2, 1, 3):
        go(act_copies[r])
    local[8].wait()

    def out_rows(r):
        return pout[pl.ds(pl.multiple_of(lax.rem(x + r, NX) * PART, PART), PART), :]

    value = dot(actbuf[0], out_rows(0))
    for r in (1, 3, 2):
        act_copies[NX - r].wait_recv()
        value = value + dot(actbuf[r], out_rows(r))
    second[...] = value
    lane = iota((ROWS, HD), 1)
    inner = jnp.sum(value * tf, axis=1, keepdims=True)
    square_z = jnp.sum(value * value, axis=1, keepdims=True)
    square_f = jnp.sum(tf * tf, axis=1, keepdims=True)
    stat = jnp.where(lane == 0, inner, jnp.where(lane == 1, square_z, jnp.where(lane == 2, square_f, 0.0)))
    sstat[...] = stat.T[0:8]
    s_copies = x_copies(4, lambda r: sstat, lambda r: sstat_in.at[r])
    for r in (2, 1, 3):
        go(s_copies[r])
    for r in (1, 2, 3):
        s_copies[NX - r].wait_recv()
    stat = sstat[...]
    for r in (1, 2, 3):
        stat = stat + sstat_in[r]
    norm_z = jnp.sqrt(stat[1:2] + 1e-6)
    norm_f = jnp.sqrt(stat[2:3] + 1e-6)
    aligned = stat[0:1] / (norm_z * norm_f)
    al_ref[...] = aligned
    weight = aw_ref[...]
    rows = jnp.where(row8 == 0, -weight / (norm_z * norm_f),
                     jnp.where(row8 == 1, weight * aligned / (norm_z * norm_z), 0.0))
    cols = jnp.concatenate([rows, pad], axis=0).T
    back[...] = (cols[:, 0:1] * tf + cols[:, 1:2] * second[...]).astype(BF16)

    u_copies = x_copies(5, lambda r: fsend.at[1, r], lambda r: frecv.at[1, r])
    for r in (2, 1, 3, 0):
        fsend[1, r] = dot(back[...], out_rows(r), 1, 1).astype(BF16)
        if r:
            go(u_copies[r])

    def reduction(n, left, right, xs, xr, hs, yr, zs, zr, out):
        def across(jj):
            return rcopy(xs.at[jj], xr.at[jj], gx_s.at[n, jj], gx_r.at[n, jj], {"section": 1 - sec})

        def y_copy(r):
            peer = lax.rem(y + r, NY)
            return rcopy(hs.at[peer], yr.at[NY - r], gy_s.at[n, r - 1], gy_r.at[n, NY - r - 1],
                         {"seq": peer * NZ + z})

        def z_copy(r):
            peer = lax.rem(z + r, NZ)
            return rcopy(zs.at[peer], zr.at[NZ - r], gz_s.at[n, r - 1], gz_r.at[n, NZ - r - 1],
                         {"seq": y * NZ + peer})

        def product(j):
            return dot(left[lax.rem(j + NX - x, NX)], right[...], 0, 0).astype(BF16)

        def start():
            for jj in range(2):
                xs[jj] = product(2 * (1 - sec) + jj)
                go(across(jj))
            for jj in range(2):
                value = product(2 * sec + jj)
                for b in range(2):
                    hs[2 * jj + b] = value[b * 256:(b + 1) * 256]

        def middle():
            for jj in range(2):
                across(jj).wait_recv()
                for b in range(2):
                    hs[2 * jj + b] = (hs[2 * jj + b].astype(F32)
                                      + xr[jj, b * 256:(b + 1) * 256].astype(F32)).astype(BF16)
            for r in (2, 1, 3):
                go(y_copy(r))

        def late():
            for r in (1, 2, 3):
                y_copy(NY - r).wait_recv()
            value = hs[y].astype(F32)
            for r in (1, 2, 3):
                value = value + yr[r].astype(F32)
            zs[...] = value.astype(BF16).reshape(zs.shape)
            for r in (4, 3, 5, 2, 6, 1, 7):
                go(z_copy(r))

        def end():
            for r in range(1, NZ):
                z_copy(NZ - r).wait_recv()
            value = zs[z].astype(F32)
            for r in range(1, NZ):
                value = value + zr[r].astype(F32)
            out[...] = value

        return start, middle, late, end

    go_steps = reduction(0, actbuf, back, go_x, go_xr, go_h, go_yr, go_z, go_zr, go_ref)
    gi_steps = reduction(1, dbuf, hidden, gi_x, gi_xr, gi_h, gi_yr, gi_z, gi_zr, gi_ref)
    go_steps[0]()

    upstream = x_sum(1, u_copies)
    value = first[...]
    sig = jax.nn.sigmoid(value)
    dbuf[0] = (upstream * sig * (1.0 + value * (1.0 - sig))).astype(BF16)
    d_copies = x_copies(6, lambda r: dbuf.at[0], lambda r: dbuf.at[r])
    for r in (2, 1, 3):
        go(d_copies[r])
    go_steps[1]()
    for r in (1, 2, 3):
        d_copies[NX - r].wait_recv()
    gi_steps[0]()
    go_steps[2]()
    gi_steps[1]()
    go_steps[3]()
    gi_steps[2]()
    gi_steps[3]()

    for copy in pending:
        copy.wait_send()

    def sent_rows(i, c):
        row_copy(lax.rem(seq + i, NSEQ), seq).wait_send()
        return c

    lax.fori_loop(1, NSEQ, sent_rows, 0)


def body(
    queries, keys, values, residual, segment_ids, enc_counts, enc_hidden, enc_down, enc_resid,
    layer_scale, norm_gain, norm_bias, proj_in, proj_out, align_weight,
):
    anywhere = pl.BlockSpec(memory_space=pl.ANY)
    vmem = pl.BlockSpec(memory_space=pltpu.VMEM)
    V, D = pltpu.VMEM, pltpu.SemaphoreType.DMA
    scratch = [
        V((NZ, ROWS, WIDTH), BF16), V((NY, ROWS, WIDTH), BF16), V((NY, ROWS, WIDTH), BF16),
        V((WIDTH, NY * ROWS), BF16), V((NY, ROWS, HD), BF16), V((ROWS, WIDTH), BF16),
        V((CAP, FF), BF16), V((FF, ENC_D), BF16), V((CAP, CH), BF16),
        V((WIDTH, PROJ), BF16), V((PROJ, CH), BF16),
        V((NZ, 2, HALF, HD), BF16), V((NZ, 2, 8, HD), F32),
        V((2, 4, 2, HALF, HD), BF16), V((2, 4, 2, 8, HD), F32),
        V((NX, CAP, CH), BF16), V((NX, CAP, CH), BF16), V((CAP, CH), F32),
        V((8, CAP), F32), V((NX, 8, CAP), F32),
        V((NSEQ, 8, CH), F32), V((NSEQ, 8, CH), F32), V((ROWS, CH), F32),
        V((ROWS, WIDTH), BF16), V((2, NX, ROWS, PART), BF16), V((2, NX, ROWS, PART), BF16),
        V((ROWS, PART), F32), V((NX, ROWS, PART), BF16), V((ROWS, CH), F32),
        V((8, ROWS), F32), V((NX, 8, ROWS), F32), V((ROWS, CH), BF16), V((NX, ROWS, PART), BF16),
        V((2, HD, HD), F32),
    ]
    for width in (CH, WIDTH):
        scratch += [
            V((2, PART, width), BF16), V((2, PART, width), BF16), V((NY, 256, width), BF16),
            V((NY, 256, width), BF16), V((NZ, 32, width), BF16), V((NZ, 32, width), BF16),
        ]
    scratch += [
        D((9,)), D((2, 4)), D((2, 4)), D((6,)), D((6,)), D((2, 4)), D((2, 4)), D((2, 4)), D((2, 4)),
        D((7, 3)), D((7, 3)), D((NSEQ,)), D((NSEQ,)),
        D((2, 2)), D((2, 2)), D((2, 3)), D((2, 3)), D((2, 7)), D((2, 7)),
    ]
    aligned, grad_in_t, grad_out = pl.pallas_call(
        kernel,
        out_shape=(
            jax.ShapeDtypeStruct((1, ROWS), F32),
            jax.ShapeDtypeStruct((32, WIDTH), F32),
            jax.ShapeDtypeStruct((32, CH), F32),
        ),
        in_specs=[anywhere] * 4 + [vmem] * 2 + [anywhere] * 3 + [vmem] * 3 + [anywhere] * 2 + [vmem],
        out_specs=(vmem, vmem, vmem),
        scratch_shapes=scratch,
        compiler_params=pltpu.CompilerParams(
            collective_id=0, has_side_effects=True, vmem_limit_bytes=56 * 1024 * 1024
        ),
        name="align",
    )(
        queries, keys, values, residual, segment_ids, enc_counts, enc_hidden, enc_down, enc_resid,
        layer_scale.reshape(1, -1), norm_gain.reshape(1, -1), norm_bias.reshape(1, -1),
        proj_in, proj_out, align_weight.reshape(1, -1),
    )
    return aligned.reshape(-1), grad_in_t, grad_out


def solution(mesh):
    return jax.shard_map(
        body,
        mesh=mesh,
        in_specs=(
            P(("section", "seq"), "mp"),
            P(("section", "seq"), "mp"),
            P(("section", "seq"), "mp"),
            P(("section", "seq"), "mp"),
            P("section", None),
            P("section", None),
            P(("section", "seq"), "mp"),
            P("mp", None),
            P(("section", "seq"), "mp"),
            P(),
            P(),
            P(),
            P("mp", None),
            P(None, "mp"),
            P(("section", "seq")),
        ),
        out_specs=(P(("section", "seq")), P(("section", "seq"), "mp"), P(("section", "seq"), "mp")),
        check_vma=False,
    )
```

time: 666 us -> 142 us (0.21)
  waiting for transfers between devices: 515 us -> 0 us
  Pallas kernels: 0 us -> 133 us
  local copies, waits for them, and re-layouts: 61.1 us -> 7.97 us
  matrix products: 35.6 us -> 0 us
  between operations: 17.5 us -> 0.64 us
  blocking collectives: 14.4 us -> 0 us
  other arithmetic: 7.58 us -> 0 us
    reduce_scatter x2 -> x0, waiting for transfers between devices: 289 us -> none  [the longest x1 151 us: body(): lax.psum_scatter(lax.dot_general(dfirst, hidden, (((0,), (0,)), ((), ()))...]
    pallas_call x0 -> x1, Pallas kernels: none -> 133 us  [body(): pl.pallas_call(kernel, out_shape=(jax.ShapeDtypeStruct((1, ROWS), F32), j...]
    all_gather x2 -> x0, waiting for transfers between devices: 125 us -> none  [the longest x1 66.8 us: body(): value_piece = lax.all_gather(values, 'seq', axis=0, tiled=True)]
    psum x2 -> x0, waiting for transfers between devices: 73.8 us -> none  [the longest x1 46.5 us: body(): lax.psum(lax.dot_general(back, proj_out, (((1,), (1,)), ((), ())), prefer...]
    dot_general x14 -> x0, matrix products: 35.6 us -> none  [the longest x4 11.3 us: one_block(): jnp.einsum('hqk,khd->hqd', weights.astype(jnp.bfloat16), value_block, pre...]
    reshape x4 -> x3, local copies, waits for them, and re-layouts: 28.2 us -> 3.88 us  [the longest x1 1.3 us: body(): layer_scale.reshape(1, -1)]
    unnamed x8 -> x0, waiting for transfers between devices: 19.4 us -> none
    unnamed x30 -> x3, local copies, waits for them, and re-layouts: 20.6 us -> 4.09 us
  transfers between devices with their start and end apart: 8 -> 0, of which waited for: 8 -> 0; matrix products, arithmetic and copies ran while one was open for 6% -> 0% of each run, Pallas kernels for 0% -> 0%
where the time goes in v1:
time: 142 us
  Pallas kernels  133 us (94%)
  local copies, waits for them, and re-layouts  7.97 us (6%)
    pallas_call x1, Pallas kernels, body(): pl.pallas_call(kernel, out_shape=(jax.ShapeDtypeStruct((1, ROWS), F32), j...  133 us
    unnamed x3, local copies, waits for them, and re-layouts  4.09 us

profile of v1, /device:TPU:1, one launch (start us, length us, event | category | flops | bytes accessed | tf_op | source)
XLA Modules:
  0.0 142.0 jit_solution(6538879190321131310)
XLA Ops:
  0.6 1.3 reshape.21.ls_ref
  1.9 1.3 reshape.22.gain_ref
  3.2 1.3 reshape.23.bias_ref
  4.5 133.4 %align.1 = (f32[1,128]{1,0:T(1,128)}, f32[32,768]{1,0:T(8,128)}, f32[32,384]{1,0:T(8,128)}) custom-call(bf16[128,768]{1,0:T(8,128)(2,1)} %q_hbm.1, bf16[128,768]{1,0:T(8,128)(2,1)} %k_hbm.1, bf16[128,768]{1,0:T(8,128)(2,1)} %v_hbm.1, bf16[128,768]{1,0:T(8,128)(2,1)} %res_hbm.1, s32[1,4096]{1,0:T(1,128)} %seg_ref.1, s32[1,32]{1,0:T(1,128)} %cnt_ref.1, ...), custom_call_target="tpu_custom_call" | custom-call | tf_op jit(solution)/shard_map/align/pallas_call | solution.py:507
  137.9 1.1 copy.21
  139.0 1.5 %copy.22 = f32[32,768]{1,0:T(8,128)} copy(f32[32,768]{1,0:T(8,128)} %get-tuple-element.13) | data formatting | bytes 196608
  140.6 1.4 %copy.23 = f32[32,384]{1,0:T(8,128)} copy(f32[32,384]{1,0:T(8,128)} %get-tuple-element.14) | data formatting | bytes 98304

commit v2 on v1

--- a/solution.py
+++ b/solution.py
@@ -46,12 +46,12 @@
     al_ref, gi_ref, go_ref,
     qbuf, kbuf, vbuf, vt, ko, resv, ehv, edv, erv, pin, pout,
     opart, stats, oin, sin,
-    esend, erecv, share, estat, estat_in, packed, arecv, target,
+    esend, erecv, share, estat, estat_in, packed, arecv, aturn, alast, target,
     hidden, fsend, frecv, first, actbuf, second, sstat, sstat_in, back, dbuf, segrow,
     go_x, go_xr, go_h, go_yr, go_z, go_zr,
-    gi_x, gi_xr, gi_h, gi_yr, gi_z, gi_zr,
-    lsem, q_s, q_r, kv_s, kv_r, o_s, o_r, os_s, os_r, x_s, x_r, a_s, a_r,
-    gx_s, gx_r, gy_s, gy_r, gz_s, gz_r,
+    gi_x, gi_xr, gi_h, a_y, a_yr, a_z, a_zr, b_z, b_in, b_y, b_yr,
+    lsem, q_s, q_r, kv_s, kv_r, o_s, o_r, os_s, os_r, x_s, x_r, ay_s, ay_r, az_s, az_r,
+    gx_s, gx_r, gy_s, gy_r, gz_s, gz_r, gb_s, gb_r,
 ):
     sec = lax.axis_index("section")
     seq = lax.axis_index("seq")
@@ -69,6 +69,9 @@
         pending.append(copy)
         return copy
 
+    def take(copy):
+        copy.wait_recv()
+
     local = []
     for n, (src, dst) in enumerate((
         (q_hbm, qbuf.at[0]), (k_hbm, kbuf.at[0]), (v_hbm, vbuf.at[0]), (eh_hbm, ehv), (ed_hbm, edv),
@@ -80,24 +83,19 @@
 
     barrier = pltpu.get_barrier_semaphore()
 
-    def greet(i, c):
-        pl.semaphore_signal(barrier, inc=1, device_id={"seq": lax.rem(seq + i, NSEQ)}, device_id_type=MESH)
-        return c
-
-    lax.fori_loop(1, NSEQ, greet, 0)
-    for r in range(1, NX):
-        pl.semaphore_signal(barrier, inc=1, device_id={"mp": lax.rem(x + r, NX)}, device_id_type=MESH)
-    pl.semaphore_signal(barrier, inc=1, device_id={"section": 1 - sec}, device_id_type=MESH)
-    pl.semaphore_wait(barrier, NSEQ - 1 + NX - 1 + 1)
-
-    def q_copy(d, t):
-        slot = (8 - t) % 8 if d == 0 else t
-        to = 7 - t if d == 0 else t + 1
-        src, dst = qbuf.at[slot], qbuf.at[to]
-        if t == 3:
-            cols = pl.ds(d * HALF, HALF)
-            src, dst = qbuf.at[slot, :, cols], qbuf.at[to, :, cols]
-        return rcopy(src, dst, q_s.at[d, t], q_r.at[d, t], zp if d == 0 else zm)
+    greeted = [{"seq": y * NZ + lax.rem(z + r, NZ)} for r in range(1, NZ)]
+    greeted += [{"seq": lax.rem(y + r, NY) * NZ + z} for r in range(1, NY)]
+    greeted += [{"mp": lax.rem(x + r, NX)} for r in range(1, NX)]
+    greeted += [{"section": 1 - sec}]
+    for device in greeted:
+        pl.semaphore_signal(barrier, inc=1, device_id=device, device_id_type=MESH)
+    pl.semaphore_wait(barrier, len(greeted))
+
+    def q_copy(d, t, half):
+        cols = pl.ds(half * HALF, HALF)
+        src = qbuf.at[(8 - t) % 8 if d == 0 else t, :, cols]
+        dst = qbuf.at[7 - t if d == 0 else t + 1, :, cols]
+        return rcopy(src, dst, q_s.at[d, t, half], q_r.at[d, t, half], zp if d == 0 else zm)
 
     def kv_copy(n):
         src, dst, dev = (
@@ -107,11 +105,12 @@
         )[n]
         return rcopy(src, dst, kv_s.at[n], kv_r.at[n], dev)
 
-    q_copies = [[q_copy(d, t) for t in range(4)] for d in range(2)]
+    q_copies = [[{h: q_copy(d, t, h) for h in ((0, 1) if t < 3 else (d,))} for t in range(4)] for d in range(2)]
     kv_copies = [kv_copy(n) for n in range(6)]
     local[0].wait()
-    go(q_copies[0][0])
-    go(q_copies[1][0])
+    for half in range(2):
+        for d in range(2):
+            go(q_copies[d][0][half])
     local[1].wait()
     go(kv_copies[0])
     go(kv_copies[1])
@@ -152,25 +151,29 @@
         device = lax.rem(y + r, NY) * NZ + z
         ko[r] = jnp.where(image_columns(device), SAME, 0.0).astype(BF16)
 
-    def forward_q(t):
+    def forward_q(t, half):
         for d in range(2):
-            q_copies[d][t].wait_recv()
-            if t < 3:
-                go(q_copies[d][t + 1])
-
-    forward_q(0)
-    kv_copies[0].wait_recv()
+            if half in q_copies[d][t]:
+                take(q_copies[d][t][half])
+            if t < 3 and half in q_copies[d][t + 1]:
+                go(q_copies[d][t + 1][half])
+
+    forward_q(0, 0)
+    forward_q(0, 1)
+    take(kv_copies[0])
     go(kv_copies[4])
-    kv_copies[1].wait_recv()
+    take(kv_copies[1])
 
     local[5].wait()
-    own = pl.ds(pl.multiple_of(x * CH, CH), CH)
-    for r in (1, 2, 3):
-        enc_copies[NX - r].wait_recv()
+    def own(ref):
+        return jnp.concatenate([ref[pl.ds(3 * x + i, 1), :] for i in range(3)], axis=1)
+
+    for r in (1, 2, 3):
+        take(enc_copies[NX - r])
     enc = esend[0].astype(F32)
     for r in (1, 2, 3):
         enc = enc + erecv[r].astype(F32)
-    enc = erv[...].astype(F32) + ls_ref[:, own] * enc
+    enc = erv[...].astype(F32) + own(ls_ref) * enc
     share[...] = enc
     lane = iota((CAP, HD), 1)
     total = jnp.sum(enc, axis=1, keepdims=True)
@@ -182,13 +185,14 @@
     for r in (2, 1, 3):
         go(stat_copies[r])
 
-    kv_copies[2].wait_recv()
-    kv_copies[3].wait_recv()
+    take(kv_copies[2])
+    take(kv_copies[3])
     go(kv_copies[5])
-    forward_q(1)
-
-    for r in (1, 2, 3):
-        stat_copies[NX - r].wait_recv()
+    forward_q(1, 0)
+    forward_q(1, 1)
+
+    for r in (1, 2, 3):
+        take(stat_copies[NX - r])
     both = estat[...]
     for r in (1, 2, 3):
         both = both + estat_in[r]
@@ -196,8 +200,8 @@
     scale = lax.rsqrt(both[1:2] * (1.0 / ENC_D) - mean * mean + 1e-6)
     pad = jnp.zeros((HD - 8, HD), F32)
     row8 = iota((8, HD), 0)
-    gain = gain_ref[:, own]
-    bias = bias_ref[:, own]
+    gain = own(gain_ref)
+    bias = own(bias_ref)
     parts = []
     for b in range(2):
         cut = slice(b * HD, (b + 1) * HD)
@@ -210,20 +214,23 @@
     row = iota((CAP, CAP), 0)
     wanted = (row & 7) * NSEQ + (((row >> 3) - before) & (NSEQ - 1))
     permutation = jnp.where(iota((CAP, CAP), 1) == wanted, 1.0, 0.0).astype(BF16)
-    packed[...] = dot(permutation, feature).reshape(NSEQ, 8, CH)
-
-    def row_copy(peer, mine):
-        return rcopy(packed.at[peer], arecv.at[mine], a_s.at[peer], a_r.at[mine], {"seq": peer})
-
-    def send_rows(i, c):
-        row_copy(lax.rem(seq + i, NSEQ), seq).start()
-        return c
-
-    lax.fori_loop(1, NSEQ, send_rows, 0)
-    arecv[pl.ds(seq, 1)] = packed[pl.ds(seq, 1)]
-
+    packed[...] = dot(permutation, feature).reshape(NY, NZ, 8, CH)
+
+    def row_y(r):
+        peer = lax.rem(y + r, NY)
+        return rcopy(packed.at[peer], arecv.at[y], ay_s.at[r - 1], ay_r.at[NY - r - 1], {"seq": peer * NZ + z})
+
+    def row_z(r):
+        peer = lax.rem(z + r, NZ)
+        return rcopy(aturn.at[peer], alast.at[z], az_s.at[r - 1], az_r.at[NZ - r - 1], {"seq": y * NZ + peer})
+
+    row_ys = {r: row_y(r) for r in range(1, NY)}
+    row_zs = {r: row_z(r) for r in range(1, NZ)}
+    for r in (2, 1, 3):
+        go(row_ys[r])
+    arecv[pl.ds(y, 1)] = packed[pl.ds(y, 1)]
     for n in (4, 5):
-        kv_copies[n].wait_recv()
+        take(kv_copies[n])
     for r in range(NY):
         vt[:, r * ROWS:(r + 1) * ROWS] = vbuf[r].T
     keys_image = ko[...].reshape(NY * ROWS, HD)
@@ -242,30 +249,37 @@
             stats[r, half, 3 + i:4 + i] = jnp.sum(prob, axis=0, keepdims=True)
             opart[r, half, i * HD:(i + 1) * HD] = dot(vt[cols], prob.astype(BF16)).astype(BF16)
 
-    def o_copy(d, t):
+    def o_copy(d, t, half):
         r = 4 - t if d == 0 else 4 + t
         dev = zp if d == 0 else zm
-        src, dst, ssrc, sdst = opart.at[r], oin.at[d, t], stats.at[r], sin.at[d, t]
-        if t == 0:
-            src, dst, ssrc, sdst = src.at[d], dst.at[d], ssrc.at[d], sdst.at[d]
-        return (rcopy(src, dst, o_s.at[d, t], o_r.at[d, t], dev),
-                rcopy(ssrc, sdst, os_s.at[d, t], os_r.at[d, t], dev))
-
-    o_copies = [[o_copy(d, t) for t in range(4)] for d in range(2)]
+        return (rcopy(opart.at[r, half], oin.at[d, t, half], o_s.at[d, t, half], o_r.at[d, t, half], dev),
+                rcopy(stats.at[r, half], sin.at[d, t, half], os_s.at[d, t, half], os_r.at[d, t, half], dev))
+
+    o_copies = [[{h: o_copy(d, t, h) for h in ((0, 1) if t else (d,))} for t in range(4)] for d in range(2)]
+
+    def go_o(d, t, half):
+        for copy in o_copies[d][t][half]:
+            go(copy)
+
+    def take_o(d, t, half):
+        for copy in o_copies[d][t][half]:
+            take(copy)
 
     def attend_some(i, c):
         attend(4 + (2 - i // 2) * (1 - 2 * lax.rem(i, 2)))
         return c
 
     lax.fori_loop(0, 2, attend_some, 0)
-    forward_q(2)
+    forward_q(2, 0)
+    forward_q(2, 1)
     lax.fori_loop(2, 4, attend_some, 0)
-    forward_q(3)
+    forward_q(3, 0)
+    forward_q(3, 1)
     lax.fori_loop(4, 5, attend_some, 0)
     for d in range(2):
-        for copy in o_copies[d][0]:
-            go(copy)
-
+        go_o(d, 0, d)
+    for d in range(2):
+        go_o(d, 1, 1 - d)
     def merge(r, d, t, half):
         mine, other = stats[r, half], sin[d, t, half]
         for i in range(3):
@@ -279,24 +293,30 @@
             stats[r, half, 3 + i:4 + i] = mine[3 + i:4 + i] * f0 + other[3 + i:4 + i] * f1
 
     for t in (1, 2, 3):
-        if t > 1:
+        if t < 3:
             def attend_rest(i, c):
-                attend(lax.rem(7 + 2 * i, 8) if t == 2 else 0 * i)
+                attend(lax.rem(7 + 2 * i, 8) if t == 1 else 0 * i)
                 return c
-            lax.fori_loop(0, 2 if t == 2 else 1, attend_rest, 0)
+            lax.fori_loop(0, 2 if t == 1 else 1, attend_rest, 0)
+        for turn in range(2):
+            for d in range(2):
+                half = d if turn else 1 - d
+                if t == 1 and not turn:
+                    continue
+                take_o(d, t - 1, half)
+                merge(4 - t if d == 0 else 4 + t, d, t - 1, half)
+                go_o(d, t, half)
+    for r in (1, 2, 3):
+        take(row_ys[NY - r])
+    for n in range(NZ):
+        aturn[n] = arecv[:, n].reshape(NY * 8, CH).astype(BF16)
+    alast[pl.ds(z, 1)] = aturn[pl.ds(z, 1)]
+    for half in range(2):
         for d in range(2):
-            for copy in o_copies[d][t - 1]:
-                copy.wait_recv()
-            for half in range(2):
-                if t > 1 or half == d:
-                    merge(4 - t if d == 0 else 4 + t, d, t - 1, half)
-            for copy in o_copies[d][t]:
-                go(copy)
-    for d in range(2):
-        for copy in o_copies[d][3]:
-            copy.wait_recv()
-        for half in range(2):
+            take_o(d, 3, half)
             merge(0, d, 3, half)
+    for r in (4, 3, 5, 2, 6, 1, 7):
+        go(row_zs[r])
     local[6].wait()
     for h in range(HEADS):
         half, i = h // 3, h % 3
@@ -313,7 +333,24 @@
         if r:
             go(f_copies[r])
 
-    e_of = iota((NSEQ, CAP), 1) >> 3
+    def x_sum(phase, copies):
+        for r in (1, 2, 3):
+            take(copies[NX - r])
+        value = fsend[phase, 0].astype(F32)
+        for r in (1, 2, 3):
+            value = value + frecv[phase, r].astype(F32)
+        return value
+
+    value = x_sum(0, f_copies)
+    first[...] = value
+    actbuf[0] = (value * jax.nn.sigmoid(value)).astype(BF16)
+    act_copies = x_copies(3, lambda r: actbuf.at[0], lambda r: actbuf.at[r])
+    for r in (2, 1, 3):
+        go(act_copies[r])
+    local[8].wait()
+
+    column = iota((NSEQ, CAP), 1)
+    e_of = ((column >> 3) & (NY - 1)) * NZ + (column >> 5)
     device = iota((NSEQ, CAP), 0)
     counts8 = jnp.broadcast_to(counts, (8, NSEQ)).astype(BF16)
     start = dot(counts8, jnp.where(device < e_of, 1.0, 0.0).astype(BF16))[0:1]
@@ -323,37 +360,17 @@
     place = (iota((ROWS, CAP), 0) * NSEQ + seq).astype(F32)
     chosen = jnp.where((place >= low) & (place < high), 1.0, 0.0).astype(BF16)
 
-    def take_rows(i, c):
-        peer = lax.rem(seq + i, NSEQ)
-        row_copy(seq, peer).wait_recv()
-        return c
-
-    lax.fori_loop(1, NSEQ, take_rows, 0)
-    target[...] = dot(chosen, arecv[...].reshape(CAP, CH).astype(BF16))
+    for r in range(1, NZ):
+        take(row_zs[NZ - r])
+    target[...] = dot(chosen, alast[...].reshape(CAP, CH))
     tf = target[...]
-
-    def x_sum(phase, copies):
-        for r in (1, 2, 3):
-            copies[NX - r].wait_recv()
-        value = fsend[phase, 0].astype(F32)
-        for r in (1, 2, 3):
-            value = value + frecv[phase, r].astype(F32)
-        return value
-
-    value = x_sum(0, f_copies)
-    first[...] = value
-    actbuf[0] = (value * jax.nn.sigmoid(value)).astype(BF16)
-    act_copies = x_copies(3, lambda r: actbuf.at[0], lambda r: actbuf.at[r])
-    for r in (2, 1, 3):
-        go(act_copies[r])
-    local[8].wait()
 
     def out_rows(r):
         return pout[pl.ds(pl.multiple_of(lax.rem(x + r, NX) * PART, PART), PART), :]
 
     value = dot(actbuf[0], out_rows(0))
     for r in (1, 3, 2):
-        act_copies[NX - r].wait_recv()
+        take(act_copies[NX - r])
         value = value + dot(actbuf[r], out_rows(r))
     second[...] = value
     lane = iota((ROWS, HD), 1)
@@ -366,7 +383,7 @@
     for r in (2, 1, 3):
         go(s_copies[r])
     for r in (1, 2, 3):
-        s_copies[NX - r].wait_recv()
+        take(s_copies[NX - r])
     stat = sstat[...]
     for r in (1, 2, 3):
         stat = stat + sstat_in[r]
@@ -400,13 +417,17 @@
             return rcopy(zs.at[peer], zr.at[NZ - r], gz_s.at[n, r - 1], gz_r.at[n, NZ - r - 1],
                          {"seq": y * NZ + peer})
 
+        acrosses = [across(jj) for jj in range(2)]
+        y_copies = {r: y_copy(r) for r in range(1, NY)}
+        z_copies = {r: z_copy(r) for r in range(1, NZ)}
+
         def product(j):
             return dot(left[lax.rem(j + NX - x, NX)], right[...], 0, 0).astype(BF16)
 
         def start():
             for jj in range(2):
                 xs[jj] = product(2 * (1 - sec) + jj)
-                go(across(jj))
+                go(acrosses[jj])
             for jj in range(2):
                 value = product(2 * sec + jj)
                 for b in range(2):
@@ -414,26 +435,26 @@
 
         def middle():
             for jj in range(2):
-                across(jj).wait_recv()
+                take(acrosses[jj])
                 for b in range(2):
                     hs[2 * jj + b] = (hs[2 * jj + b].astype(F32)
                                       + xr[jj, b * 256:(b + 1) * 256].astype(F32)).astype(BF16)
             for r in (2, 1, 3):
-                go(y_copy(r))
+                go(y_copies[r])
 
         def late():
             for r in (1, 2, 3):
-                y_copy(NY - r).wait_recv()
+                take(y_copies[NY - r])
             value = hs[y].astype(F32)
             for r in (1, 2, 3):
                 value = value + yr[r].astype(F32)
             zs[...] = value.astype(BF16).reshape(zs.shape)
             for r in (4, 3, 5, 2, 6, 1, 7):
-                go(z_copy(r))
+                go(z_copies[r])
 
         def end():
             for r in range(1, NZ):
-                z_copy(NZ - r).wait_recv()
+                take(z_copies[NZ - r])
             value = zs[z].astype(F32)
             for r in range(1, NZ):
                 value = value + zr[r].astype(F32)
@@ -442,7 +463,6 @@
         return start, middle, late, end
 
     go_steps = reduction(0, actbuf, back, go_x, go_xr, go_h, go_yr, go_z, go_zr, go_ref)
-    gi_steps = reduction(1, dbuf, hidden, gi_x, gi_xr, gi_h, gi_yr, gi_z, gi_zr, gi_ref)
     go_steps[0]()
 
     upstream = x_sum(1, u_copies)
@@ -454,22 +474,110 @@
         go(d_copies[r])
     go_steps[1]()
     for r in (1, 2, 3):
-        d_copies[NX - r].wait_recv()
-    gi_steps[0]()
+        take(d_copies[NX - r])
+
+    def across(jj):
+        return rcopy(gi_x.at[jj], gi_xr.at[jj], gx_s.at[1, jj], gx_r.at[1, jj], {"section": 1 - sec})
+
+    def product(j):
+        return dot(dbuf[lax.rem(j + NX - x, NX)], hidden[...], 0, 0).astype(BF16)
+
+    def ya_copy(r):
+        peer = lax.rem(y + r, NY)
+        return rcopy(a_y.at[peer], a_yr.at[NY - r], gy_s.at[1, r - 1], gy_r.at[1, NY - r - 1], {"seq": peer * NZ + z})
+
+    def za_copy(r):
+        peer = lax.rem(z + r, NZ)
+        return rcopy(a_z.at[peer], a_zr.at[NZ - r], gz_s.at[1, r - 1], gz_r.at[1, NZ - r - 1], {"seq": y * NZ + peer})
+
+    def yb_copy(r):
+        peer = lax.rem(y + r, NY)
+        return rcopy(b_y.at[peer], b_yr.at[NY - r], gy_s.at[2, r - 1], gy_r.at[2, NY - r - 1], {"seq": peer * NZ + z})
+
+    def zb_copy(d, t, half):
+        chunk = lax.rem(z + (4 - t if d == 0 else 4 + t), NZ)
+        part = pl.ds(2 * half, 2)
+        return rcopy(b_z.at[chunk, part], b_in.at[d, t, part], gb_s.at[d, t, half], gb_r.at[d, t, half],
+                     zp if d == 0 else zm)
+
+    acrosses = [across(jj) for jj in range(2)]
+    ya_copies = {r: ya_copy(r) for r in range(1, NY)}
+    za_copies = {r: za_copy(r) for r in range(1, NZ)}
+    yb_copies = {r: yb_copy(r) for r in range(1, NY)}
+    zb_copies = [[{h: zb_copy(d, t, h) for h in ((0, 1) if t else (d,))} for t in range(4)] for d in range(2)]
+    for jj in range(2):
+        gi_x[jj] = product(2 * (1 - sec) + jj)
+        go(acrosses[jj])
     go_steps[2]()
-    gi_steps[1]()
+    for jj in range(2):
+        gi_h[jj] = product(2 * sec + jj)
+    for jj in range(2):
+        take(acrosses[jj])
+        for b in range(2):
+            rows = slice(b * 256, (b + 1) * 256)
+            value = (gi_h[jj, rows].astype(F32) + gi_xr[jj, rows].astype(F32)).astype(BF16)
+            a_y[2 * jj + b] = value[:, 0:HALF]
+            for n in range(NZ):
+                b_z[n, 2 * jj + b] = value[n * 32:(n + 1) * 32, HALF:WIDTH]
+
+    def go_b(d, t, half):
+        go(zb_copies[d][t][half])
+
+    def merge_b(d, t, half):
+        take(zb_copies[d][t][half])
+        chunk = lax.rem(z + (3 - t if d == 0 else 5 + t), NZ)
+        part = pl.ds(2 * half, 2)
+        b_z[chunk, part] = (b_z[chunk, part].astype(F32) + b_in[d, t, part].astype(F32)).astype(BF16)
+
+    for d in range(2):
+        go_b(d, 0, d)
+    for r in (2, 1, 3):
+        go(ya_copies[r])
+    for d in range(2):
+        go_b(d, 1, 1 - d)
+    for d in range(2):
+        merge_b(d, 0, d)
+        go_b(d, 1, d)
+    for turn in range(2):
+        for d in range(2):
+            half = d if turn else 1 - d
+            merge_b(d, 1, half)
+            go_b(d, 2, half)
+    for r in (1, 2, 3):
+        take(ya_copies[NY - r])
+    value = a_y[y].astype(F32)
+    for r in (1, 2, 3):
+        value = value + a_yr[r].astype(F32)
+    a_z[...] = value.astype(BF16).reshape(NZ, 32, HALF)
+    for r in (4, 3, 5, 2, 6, 1, 7):
+        go(za_copies[r])
+    for turn in range(2):
+        for d in range(2):
+            half = d if turn else 1 - d
+            merge_b(d, 2, half)
+            go_b(d, 3, half)
+    for half in range(2):
+        for d in range(2):
+            merge_b(d, 3, half)
+    b_y[...] = b_z[z]
+    for r in (2, 1, 3):
+        go(yb_copies[r])
     go_steps[3]()
-    gi_steps[2]()
-    gi_steps[3]()
+    for r in range(1, NZ):
+        take(za_copies[NZ - r])
+    value = a_z[z].astype(F32)
+    for r in range(1, NZ):
+        value = value + a_zr[r].astype(F32)
+    gi_ref[:, 0:HALF] = value
+    for r in (1, 2, 3):
+        take(yb_copies[NY - r])
+    value = b_y[y].astype(F32)
+    for r in (1, 2, 3):
+        value = value + b_yr[r].astype(F32)
+    gi_ref[:, HALF:WIDTH] = value
 
     for copy in pending:
         copy.wait_send()
-
-    def sent_rows(i, c):
-        row_copy(lax.rem(seq + i, NSEQ), seq).wait_send()
-        return c
-
-    lax.fori_loop(1, NSEQ, sent_rows, 0)
 
 
 def body(
@@ -488,21 +596,25 @@
         V((2, 4, 2, HALF, HD), BF16), V((2, 4, 2, 8, HD), F32),
         V((NX, CAP, CH), BF16), V((NX, CAP, CH), BF16), V((CAP, CH), F32),
         V((8, CAP), F32), V((NX, 8, CAP), F32),
-        V((NSEQ, 8, CH), F32), V((NSEQ, 8, CH), F32), V((ROWS, CH), F32),
+        V((NY, NZ, 8, CH), F32), V((NY, NZ, 8, CH), F32), V((NZ, 32, CH), BF16), V((NZ, 32, CH), BF16),
+        V((ROWS, CH), F32),
         V((ROWS, WIDTH), BF16), V((2, NX, ROWS, PART), BF16), V((2, NX, ROWS, PART), BF16),
         V((ROWS, PART), F32), V((NX, ROWS, PART), BF16), V((ROWS, CH), F32),
         V((8, ROWS), F32), V((NX, 8, ROWS), F32), V((ROWS, CH), BF16), V((NX, ROWS, PART), BF16),
         V((2, HD, HD), F32),
     ]
-    for width in (CH, WIDTH):
-        scratch += [
-            V((2, PART, width), BF16), V((2, PART, width), BF16), V((NY, 256, width), BF16),
-            V((NY, 256, width), BF16), V((NZ, 32, width), BF16), V((NZ, 32, width), BF16),
-        ]
     scratch += [
-        D((9,)), D((2, 4)), D((2, 4)), D((6,)), D((6,)), D((2, 4)), D((2, 4)), D((2, 4)), D((2, 4)),
-        D((7, 3)), D((7, 3)), D((NSEQ,)), D((NSEQ,)),
-        D((2, 2)), D((2, 2)), D((2, 3)), D((2, 3)), D((2, 7)), D((2, 7)),
+        V((2, PART, CH), BF16), V((2, PART, CH), BF16), V((NY, 256, CH), BF16),
+        V((NY, 256, CH), BF16), V((NZ, 32, CH), BF16), V((NZ, 32, CH), BF16),
+        V((2, PART, WIDTH), BF16), V((2, PART, WIDTH), BF16), V((2, PART, WIDTH), BF16),
+        V((NY, 256, HALF), BF16), V((NY, 256, HALF), BF16), V((NZ, 32, HALF), BF16), V((NZ, 32, HALF), BF16),
+        V((NZ, NY, 32, HALF), BF16), V((2, 4, NY, 32, HALF), BF16), V((NY, 32, HALF), BF16), V((NY, 32, HALF), BF16),
+    ]
+    scratch += [
+        D((9,)), D((2, 4, 2)), D((2, 4, 2)), D((6,)), D((6,)),
+        D((2, 4, 2)), D((2, 4, 2)), D((2, 4, 2)), D((2, 4, 2)),
+        D((7, 3)), D((7, 3)), D((3,)), D((3,)), D((7,)), D((7,)),
+        D((2, 2)), D((2, 2)), D((3, 3)), D((3, 3)), D((2, 7)), D((2, 7)), D((2, 4, 2)), D((2, 4, 2)),
     ]
     aligned, grad_in_t, grad_out = pl.pallas_call(
         kernel,
@@ -520,9 +632,22 @@
         name="align",
     )(
         queries, keys, values, residual, segment_ids, enc_counts, enc_hidden, enc_down, enc_resid,
-        layer_scale.reshape(1, -1), norm_gain.reshape(1, -1), norm_bias.reshape(1, -1),
+        layer_scale.reshape(-1, HD), norm_gain.reshape(-1, HD), norm_bias.reshape(-1, HD),
         proj_in, proj_out, align_weight.reshape(1, -1),
     )
+
+    def hand_on(a, b, c, a_out, b_out, c_out):
+        a_out[...] = a[...]
+        b_out[...] = b[...]
+        c_out[...] = c[...]
+
+    aligned, grad_in_t, grad_out = pl.pallas_call(
+        hand_on,
+        out_shape=tuple(jax.ShapeDtypeStruct(v.shape, F32) for v in (aligned, grad_in_t, grad_out)),
+        in_specs=[vmem] * 3,
+        out_specs=(vmem, vmem, vmem),
+        name="hand_on",
+    )(aligned, grad_in_t, grad_out)
     return aligned.reshape(-1), grad_in_t, grad_out
 
 

time: 142 us -> 124 us (0.87)
  Pallas kernels: 133 us -> 123 us
  local copies, waits for them, and re-layouts: 7.97 us -> 0 us
    pallas_call x1, Pallas kernels: 133 us -> 121 us  [body(): pl.pallas_call(kernel, out_shape=(jax.ShapeDtypeStruct((1, ROWS), F32), j...]
    unnamed x3 -> x0, local copies, waits for them, and re-layouts: 4.09 us -> none
    reshape x3 -> x0, local copies, waits for them, and re-layouts: 3.88 us -> none  [the longest x1 1.3 us: body(): layer_scale.reshape(1, -1)]
    pallas_call x0 -> x1, Pallas kernels: none -> 1.56 us  [body(): pl.pallas_call(hand_on, out_shape=tuple((jax.ShapeDtypeStruct(v.shape, F3...]
where the time goes in v2:
time: 124 us
  Pallas kernels  123 us (99%)
    pallas_call x1, Pallas kernels, body(): pl.pallas_call(kernel, out_shape=(jax.ShapeDtypeStruct((1, ROWS), F32), j...  121 us

profile of v2, /device:TPU:1, one launch (start us, length us, event | category | flops | bytes accessed | tf_op | source)
XLA Modules:
  0.0 123.5 jit_solution(2703868938769881048)
XLA Ops:
  0.6 121.3 %align.1 = (f32[1,128]{1,0:T(1,128)}, f32[32,768]{1,0:T(8,128)}, f32[32,384]{1,0:T(8,128)}) custom-call(bf16[128,768]{1,0:T(8,128)(2,1)} %q_hbm.1, bf16[128,768]{1,0:T(8,128)(2,1)} %k_hbm.1, bf16[128,768]{1,0:T(8,128)(2,1)} %v_hbm.1, bf16[128,768]{1,0:T(8,128)(2,1)} %res_hbm.1, s32[1,4096]{1,0:T(1,128)} %seg_ref.1, s32[1,32]{1,0:T(1,128)} %cnt_ref.1, ...), custom_call_target="tpu_custom_call" | custom-call | tf_op jit(solution)/shard_map/align/pallas_call | solution.py:619
  122.0 1.6 %hand_on.1 = (f32[1,128]{1,0:T(1,128)}, f32[32,768]{1,0:T(8,128)}, f32[32,384]{1,0:T(8,128)}) custom-call(f32[1,128]{1,0:T(1,128)} %get-tuple-element.9.a, f32[32,768]{1,0:T(8,128)} %get-tuple-element.10.b, f32[32,384]{1,0:T(8,128)} %get-tuple-element.11.c), custom_call_target="tpu_custom_call" | custom-call | tf_op jit(solution)/shard_map/hand_on/pallas_call | solution.py:644

commit v3 on v2

--- a/solution.py
+++ b/solution.py
@@ -44,13 +44,13 @@
     q_hbm, k_hbm, v_hbm, res_hbm, seg_ref, cnt_ref, eh_hbm, ed_hbm, er_hbm, ls_ref, gain_ref, bias_ref,
     pin_hbm, pout_hbm, aw_ref,
     al_ref, gi_ref, go_ref,
-    qbuf, kbuf, vbuf, vt, ko, resv, ehv, edv, erv, pin, pout,
+    qbuf, kbuf, vbuf, vt, ko, resv, ehv, edv, erv, pin, pfull,
     opart, stats, oin, sin,
-    esend, erecv, share, estat, estat_in, packed, arecv, aturn, alast, target,
-    hidden, fsend, frecv, first, actbuf, second, sstat, sstat_in, back, dbuf, segrow,
+    esend, erecv, share, estat, estat_in, packed, arecv, aturn, alast, tsend, tgt,
+    hidden, fpart, frecv, first, actall, second, bsend, backall, alall, dall, column_weight, segrow,
     go_x, go_xr, go_h, go_yr, go_z, go_zr,
     gi_x, gi_xr, gi_h, a_y, a_yr, a_z, a_zr, b_z, b_in, b_y, b_yr,
-    lsem, q_s, q_r, kv_s, kv_r, o_s, o_r, os_s, os_r, x_s, x_r, ay_s, ay_r, az_s, az_r,
+    lsem, q_s, q_r, kv_s, kv_r, o_s, o_r, os_s, os_r, x_s, x_r, pc_s, pc_r, ay_s, ay_r, az_s, az_r,
     gx_s, gx_r, gy_s, gy_r, gz_s, gz_r, gb_s, gb_r,
 ):
     sec = lax.axis_index("section")
@@ -75,7 +75,7 @@
     local = []
     for n, (src, dst) in enumerate((
         (q_hbm, qbuf.at[0]), (k_hbm, kbuf.at[0]), (v_hbm, vbuf.at[0]), (eh_hbm, ehv), (ed_hbm, edv),
-        (er_hbm, erv), (res_hbm, resv), (pin_hbm, pin), (pout_hbm, pout),
+        (er_hbm, erv), (res_hbm, resv), (pin_hbm, pin), (pout_hbm, pfull.at[0]),
     )):
         copy = pltpu.make_async_copy(src, dst, lsem.at[n])
         copy.start()
@@ -134,6 +134,13 @@
         if r:
             go(enc_copies[r])
 
+    local[8].wait()
+    core_rows = pl.ds(pl.multiple_of(sec * (PROJ // 2), PROJ // 2), PROJ // 2)
+    p_copies = x_copies(9, lambda r: pfull.at[0, core_rows], lambda r: pfull.at[r, core_rows])
+    pc_copies = {r: rcopy(pfull.at[r, core_rows], pfull.at[r, core_rows], pc_s.at[r - 1], pc_r.at[r - 1],
+                          {"section": 1 - sec}) for r in (1, 2, 3)}
+    for r in (1, 3, 2):
+        go(p_copies[r])
     ids = iota((16, NSEQ * ROWS), 0)
     seg = seg_ref[...]
     below = jnp.sum(jnp.where(seg < ids, 1.0, 0.0), axis=1, keepdims=True)
@@ -158,63 +165,13 @@
             if t < 3 and half in q_copies[d][t + 1]:
                 go(q_copies[d][t + 1][half])
 
-    forward_q(0, 0)
-    forward_q(0, 1)
-    take(kv_copies[0])
-    go(kv_copies[4])
-    take(kv_copies[1])
-
-    local[5].wait()
     def own(ref):
         return jnp.concatenate([ref[pl.ds(3 * x + i, 1), :] for i in range(3)], axis=1)
 
-    for r in (1, 2, 3):
-        take(enc_copies[NX - r])
-    enc = esend[0].astype(F32)
-    for r in (1, 2, 3):
-        enc = enc + erecv[r].astype(F32)
-    enc = erv[...].astype(F32) + own(ls_ref) * enc
-    share[...] = enc
-    lane = iota((CAP, HD), 1)
-    total = jnp.sum(enc, axis=1, keepdims=True)
-    square = jnp.sum(enc * enc, axis=1, keepdims=True)
-    packed_stat = jnp.where(lane == 0, total, jnp.where(lane == 1, square, 0.0))
-    for b in range(2):
-        estat[:, b * HD:(b + 1) * HD] = packed_stat[b * HD:(b + 1) * HD].T[0:8]
     stat_copies = x_copies(1, lambda r: estat, lambda r: estat_in.at[r])
-    for r in (2, 1, 3):
-        go(stat_copies[r])
-
-    take(kv_copies[2])
-    take(kv_copies[3])
-    go(kv_copies[5])
-    forward_q(1, 0)
-    forward_q(1, 1)
-
-    for r in (1, 2, 3):
-        take(stat_copies[NX - r])
-    both = estat[...]
-    for r in (1, 2, 3):
-        both = both + estat_in[r]
-    mean = both[0:1] * (1.0 / ENC_D)
-    scale = lax.rsqrt(both[1:2] * (1.0 / ENC_D) - mean * mean + 1e-6)
     pad = jnp.zeros((HD - 8, HD), F32)
     row8 = iota((8, HD), 0)
-    gain = own(gain_ref)
-    bias = own(bias_ref)
-    parts = []
-    for b in range(2):
-        cut = slice(b * HD, (b + 1) * HD)
-        rows = jnp.where(row8 == 0, mean[:, cut], jnp.where(row8 == 1, scale[:, cut], 0.0))
-        cols = jnp.concatenate([rows, pad], axis=0).T
-        parts.append((((share[cut] - cols[:, 0:1]) * cols[:, 1:2]) * gain + bias).astype(BF16))
-    feature = jnp.concatenate(parts, axis=0)
     counts = cnt_ref[...].astype(F32)
-    before = jnp.sum(jnp.where(iota((1, NSEQ), 1) < seq, counts, 0.0), axis=1, keepdims=True).astype(I32)
-    row = iota((CAP, CAP), 0)
-    wanted = (row & 7) * NSEQ + (((row >> 3) - before) & (NSEQ - 1))
-    permutation = jnp.where(iota((CAP, CAP), 1) == wanted, 1.0, 0.0).astype(BF16)
-    packed[...] = dot(permutation, feature).reshape(NY, NZ, 8, CH)
 
     def row_y(r):
         peer = lax.rem(y + r, NY)
@@ -226,18 +183,56 @@
 
     row_ys = {r: row_y(r) for r in range(1, NY)}
     row_zs = {r: row_z(r) for r in range(1, NZ)}
-    for r in (2, 1, 3):
-        go(row_ys[r])
-    arecv[pl.ds(y, 1)] = packed[pl.ds(y, 1)]
-    for n in (4, 5):
-        take(kv_copies[n])
-    for r in range(NY):
-        vt[:, r * ROWS:(r + 1) * ROWS] = vbuf[r].T
-    keys_image = ko[...].reshape(NY * ROWS, HD)
+    def sum_encoder():
+        local[5].wait()
+        for r in (1, 2, 3):
+            take(enc_copies[NX - r])
+        enc = esend[0].astype(F32)
+        for r in (1, 2, 3):
+            enc = enc + erecv[r].astype(F32)
+        enc = erv[...].astype(F32) + own(ls_ref) * enc
+        share[...] = enc
+        lane = iota((CAP, HD), 1)
+        total = jnp.sum(enc, axis=1, keepdims=True)
+        square = jnp.sum(enc * enc, axis=1, keepdims=True)
+        packed_stat = jnp.where(lane == 0, total, jnp.where(lane == 1, square, 0.0))
+        for b in range(2):
+            estat[:, b * HD:(b + 1) * HD] = packed_stat[b * HD:(b + 1) * HD].T[0:8]
+        for r in (2, 1, 3):
+            go(stat_copies[r])
+
+
+    def send_rows():
+        for r in (1, 2, 3):
+            take(stat_copies[NX - r])
+        both = estat[...]
+        for r in (1, 2, 3):
+            both = both + estat_in[r]
+        mean = both[0:1] * (1.0 / ENC_D)
+        scale = lax.rsqrt(both[1:2] * (1.0 / ENC_D) - mean * mean + 1e-6)
+        gain = own(gain_ref)
+        bias = own(bias_ref)
+        parts = []
+        for b in range(2):
+            cut = slice(b * HD, (b + 1) * HD)
+            rows = jnp.where(row8 == 0, mean[:, cut], jnp.where(row8 == 1, scale[:, cut], 0.0))
+            cols = jnp.concatenate([rows, pad], axis=0).T
+            parts.append((((share[cut] - cols[:, 0:1]) * cols[:, 1:2]) * gain + bias).astype(BF16))
+        feature = jnp.concatenate(parts, axis=0)
+        before = jnp.sum(jnp.where(iota((1, NSEQ), 1) < seq, counts, 0.0), axis=1, keepdims=True).astype(I32)
+        row = iota((CAP, CAP), 0)
+        wanted = (row & 7) * NSEQ + (((row >> 3) - before) & (NSEQ - 1))
+        permutation = jnp.where(iota((CAP, CAP), 1) == wanted, 1.0, 0.0).astype(BF16)
+        packed[...] = dot(permutation, feature).reshape(NY, NZ, 8, CH)
+
+        for r in (2, 1, 3):
+            go(row_ys[r])
+        arecv[pl.ds(y, 1)] = packed[pl.ds(y, 1)]
 
     def attend(r):
         device = y * NZ + lax.rem(z + r, NZ)
         image = jnp.where(image_columns(device), 1.0, 0.0).astype(BF16)
+        keys_image = ko[...].reshape(NY * ROWS, HD)
         for h in range(HEADS):
             cols = slice(h * HD, (h + 1) * HD)
             keys = jnp.concatenate([kbuf[:, :, cols].reshape(NY * ROWS, HD), keys_image], axis=1)
@@ -249,6 +244,19 @@
             stats[r, half, 3 + i:4 + i] = jnp.sum(prob, axis=0, keepdims=True)
             opart[r, half, i * HD:(i + 1) * HD] = dot(vt[cols], prob.astype(BF16)).astype(BF16)
 
+    def attend_two(k):
+        def one(i, c):
+            attend(4 + k * (1 - 2 * i))
+            return c
+
+        lax.fori_loop(0, 2, one, 0)
+
+    def attend_one(r):
+        lax.fori_loop(r, r + 1, lambda i, c: (attend(i), c)[1], 0)
+
+    def turn_values(r):
+        vt[:, r * ROWS:(r + 1) * ROWS] = vbuf[r].T
+
     def o_copy(d, t, half):
         r = 4 - t if d == 0 else 4 + t
         dev = zp if d == 0 else zm
@@ -265,21 +273,38 @@
         for copy in o_copies[d][t][half]:
             take(copy)
 
-    def attend_some(i, c):
-        attend(4 + (2 - i // 2) * (1 - 2 * lax.rem(i, 2)))
-        return c
-
-    lax.fori_loop(0, 2, attend_some, 0)
+    forward_q(0, 0)
+    forward_q(0, 1)
+    take(kv_copies[0])
+    go(kv_copies[4])
+    take(kv_copies[1])
+    forward_q(1, 0)
+    take(kv_copies[2])
+    take(kv_copies[3])
+    go(kv_copies[5])
+    forward_q(1, 1)
+    for r in (0, 1, 3):
+        turn_values(r)
     forward_q(2, 0)
+    sum_encoder()
     forward_q(2, 1)
-    lax.fori_loop(2, 4, attend_some, 0)
+    for n in (4, 5):
+        take(kv_copies[n])
+    turn_values(2)
+    attend_two(1)
     forward_q(3, 0)
     forward_q(3, 1)
-    lax.fori_loop(4, 5, attend_some, 0)
+    attend_one(4)
     for d in range(2):
         go_o(d, 0, d)
     for d in range(2):
         go_o(d, 1, 1 - d)
+    send_rows()
+    for r in (1, 3, 2):
+        take(p_copies[NX - r])
+        go(pc_copies[r])
+    attend_two(2)
+
     def merge(r, d, t, half):
         mine, other = stats[r, half], sin[d, t, half]
         for i in range(3):
@@ -293,11 +318,10 @@
             stats[r, half, 3 + i:4 + i] = mine[3 + i:4 + i] * f0 + other[3 + i:4 + i] * f1
 
     for t in (1, 2, 3):
-        if t < 3:
-            def attend_rest(i, c):
-                attend(lax.rem(7 + 2 * i, 8) if t == 1 else 0 * i)
-                return c
-            lax.fori_loop(0, 2 if t == 1 else 1, attend_rest, 0)
+        if t == 2:
+            attend_two(3)
+        if t == 3:
+            attend_one(0)
         for turn in range(2):
             for d in range(2):
                 half = d if turn else 1 - d
@@ -326,29 +350,14 @@
         hidden[:, cols] = (resv[:, cols].astype(F32) + attn).astype(BF16)
 
     local[7].wait()
-    f_copies = x_copies(2, lambda r: fsend.at[0, r], lambda r: frecv.at[0, r])
-    for r in (2, 1, 3, 0):
-        cols = pl.ds(pl.multiple_of(lax.rem(x + r, NX) * PART, PART), PART)
-        fsend[0, r] = dot(hidden[...], pin[:, cols]).astype(BF16)
-        if r:
-            go(f_copies[r])
-
-    def x_sum(phase, copies):
-        for r in (1, 2, 3):
-            take(copies[NX - r])
-        value = fsend[phase, 0].astype(F32)
-        for r in (1, 2, 3):
-            value = value + frecv[phase, r].astype(F32)
-        return value
-
-    value = x_sum(0, f_copies)
-    first[...] = value
-    actbuf[0] = (value * jax.nn.sigmoid(value)).astype(BF16)
-    act_copies = x_copies(3, lambda r: actbuf.at[0], lambda r: actbuf.at[r])
-    for r in (2, 1, 3):
-        go(act_copies[r])
-    local[8].wait()
-
+    f_copies = []
+    for c in range(2):
+        cols = slice(c * 1024, (c + 1) * 1024)
+        fpart[:, :, cols] = dot(hidden[...], pin[:, cols]).astype(BF16).reshape(NX, 32, 1024)
+        f_copies.append(x_copies(
+            2 + c, lambda r: fpart.at[lax.rem(x + r, NX), :, cols], lambda r: frecv.at[r, :, cols]))
+        for r in (2, 1, 3):
+            go(f_copies[c][r])
     column = iota((NSEQ, CAP), 1)
     e_of = ((column >> 3) & (NY - 1)) * NZ + (column >> 5)
     device = iota((NSEQ, CAP), 0)
@@ -362,46 +371,67 @@
 
     for r in range(1, NZ):
         take(row_zs[NZ - r])
-    target[...] = dot(chosen, alast[...].reshape(CAP, CH))
-    tf = target[...]
-
-    def out_rows(r):
-        return pout[pl.ds(pl.multiple_of(lax.rem(x + r, NX) * PART, PART), PART), :]
-
-    value = dot(actbuf[0], out_rows(0))
-    for r in (1, 3, 2):
+    tsend[...] = dot(chosen, alast[...].reshape(CAP, CH)).astype(BF16).reshape(NX, 32, CH)
+    t_copies = x_copies(5, lambda r: tsend.at[lax.rem(x + r, NX)], lambda r: tgt.at[r])
+    for r in (2, 1, 3):
+        go(t_copies[r])
+    tgt[0] = tsend[x]
+    column_weight[...] = jnp.broadcast_to(aw_ref[...], (ROWS, ROWS)).T
+    for c in range(2):
+        cols = slice(c * 1024, (c + 1) * 1024)
+        for r in (1, 2, 3):
+            take(f_copies[c][NX - r])
+        value = fpart[x, :, cols].astype(F32)
+        for r in (1, 2, 3):
+            value = value + frecv[r, :, cols].astype(F32)
+        first[:, cols] = value
+        actall[x, :, cols] = (value * jax.nn.sigmoid(value)).astype(BF16)
+    act_copies = x_copies(4, lambda r: actall.at[x], lambda r: actall.at[x])
+    for r in (2, 1, 3):
+        go(act_copies[r])
+    act = actall[x]
+    for r in range(NX):
+        if r:
+            take(pc_copies[r])
+        second[r] = dot(act, pfull[r])
+    for r in (1, 2, 3):
+        take(t_copies[NX - r])
+    inner = square_z = square_f = 0.0
+    for r in range(NX):
+        tf = tgt[r].astype(F32)
+        inner = inner + jnp.sum(second[r] * tf, axis=1, keepdims=True)
+        square_z = square_z + jnp.sum(second[r] * second[r], axis=1, keepdims=True)
+        square_f = square_f + jnp.sum(tf * tf, axis=1, keepdims=True)
+    norm_z = jnp.sqrt(square_z + 1e-6)
+    norm_f = jnp.sqrt(square_f + 1e-6)
+    aligned = inner / (norm_z * norm_f)
+    weight = column_weight[pl.ds(pl.multiple_of(x * 32, 32), 32), 0:1]
+    by_target = -weight / (norm_z * norm_f)
+    by_second = weight * aligned / (norm_z * norm_z)
+    b_copies = x_copies(6, lambda r: bsend.at[r], lambda r: backall.at[x])
+    for r in (2, 1, 3, 0):
+        bsend[r] = (by_target * tgt[r].astype(F32) + by_second * second[r]).astype(BF16)
+        if r:
+            go(b_copies[r])
+    backall[x] = bsend[0]
+    alall[x] = jnp.broadcast_to(aligned, (32, HD))
+    l_copies = x_copies(7, lambda r: alall.at[x], lambda r: alall.at[x])
+    for r in (2, 1, 3):
+        go(l_copies[r])
+    upstream = dot(bsend[0], pfull[0], 1, 1)
+    for r in (1, 2, 3):
+        upstream = upstream + dot(bsend[r], pfull[r], 1, 1)
+    value = first[...]
+    sig = jax.nn.sigmoid(value)
+    dall[x] = (upstream * sig * (1.0 + value * (1.0 - sig))).astype(BF16)
+    d_copies = x_copies(8, lambda r: dall.at[x], lambda r: dall.at[x])
+    for r in (2, 1, 3):
+        go(d_copies[r])
+    for r in (1, 2, 3):
         take(act_copies[NX - r])
-        value = value + dot(actbuf[r], out_rows(r))
-    second[...] = value
-    lane = iota((ROWS, HD), 1)
-    inner = jnp.sum(value * tf, axis=1, keepdims=True)
-    square_z = jnp.sum(value * value, axis=1, keepdims=True)
-    square_f = jnp.sum(tf * tf, axis=1, keepdims=True)
-    stat = jnp.where(lane == 0, inner, jnp.where(lane == 1, square_z, jnp.where(lane == 2, square_f, 0.0)))
-    sstat[...] = stat.T[0:8]
-    s_copies = x_copies(4, lambda r: sstat, lambda r: sstat_in.at[r])
-    for r in (2, 1, 3):
-        go(s_copies[r])
-    for r in (1, 2, 3):
-        take(s_copies[NX - r])
-    stat = sstat[...]
-    for r in (1, 2, 3):
-        stat = stat + sstat_in[r]
-    norm_z = jnp.sqrt(stat[1:2] + 1e-6)
-    norm_f = jnp.sqrt(stat[2:3] + 1e-6)
-    aligned = stat[0:1] / (norm_z * norm_f)
-    al_ref[...] = aligned
-    weight = aw_ref[...]
-    rows = jnp.where(row8 == 0, -weight / (norm_z * norm_f),
-                     jnp.where(row8 == 1, weight * aligned / (norm_z * norm_z), 0.0))
-    cols = jnp.concatenate([rows, pad], axis=0).T
-    back[...] = (cols[:, 0:1] * tf + cols[:, 1:2] * second[...]).astype(BF16)
-
-    u_copies = x_copies(5, lambda r: fsend.at[1, r], lambda r: frecv.at[1, r])
-    for r in (2, 1, 3, 0):
-        fsend[1, r] = dot(back[...], out_rows(r), 1, 1).astype(BF16)
-        if r:
-            go(u_copies[r])
+        take(b_copies[NX - r])
+        take(l_copies[NX - r])
+    al_ref[...] = alall[...].reshape(ROWS, HD).T[0:1]
 
     def reduction(n, left, right, xs, xr, hs, yr, zs, zr, out):
         def across(jj):
@@ -422,7 +452,8 @@
         z_copies = {r: z_copy(r) for r in range(1, NZ)}
 
         def product(j):
-            return dot(left[lax.rem(j + NX - x, NX)], right[...], 0, 0).astype(BF16)
+            cols = pl.ds(pl.multiple_of(j * PART, PART), PART)
+            return dot(left[:, :, cols].reshape(ROWS, PART), right[...].reshape(ROWS, -1), 0, 0).astype(BF16)
 
         def start():
             for jj in range(2):
@@ -462,16 +493,9 @@
 
         return start, middle, late, end
 
-    go_steps = reduction(0, actbuf, back, go_x, go_xr, go_h, go_yr, go_z, go_zr, go_ref)
+    go_steps = reduction(0, actall, backall, go_x, go_xr, go_h, go_yr, go_z, go_zr, go_ref)
     go_steps[0]()
 
-    upstream = x_sum(1, u_copies)
-    value = first[...]
-    sig = jax.nn.sigmoid(value)
-    dbuf[0] = (upstream * sig * (1.0 + value * (1.0 - sig))).astype(BF16)
-    d_copies = x_copies(6, lambda r: dbuf.at[0], lambda r: dbuf.at[r])
-    for r in (2, 1, 3):
-        go(d_copies[r])
     go_steps[1]()
     for r in (1, 2, 3):
         take(d_copies[NX - r])
@@ -480,7 +504,8 @@
         return rcopy(gi_x.at[jj], gi_xr.at[jj], gx_s.at[1, jj], gx_r.at[1, jj], {"section": 1 - sec})
 
     def product(j):
-        return dot(dbuf[lax.rem(j + NX - x, NX)], hidden[...], 0, 0).astype(BF16)
+        cols = pl.ds(pl.multiple_of(j * PART, PART), PART)
+        return dot(dall[:, :, cols].reshape(ROWS, PART), hidden[...], 0, 0).astype(BF16)
 
     def ya_copy(r):
         peer = lax.rem(y + r, NY)
@@ -508,7 +533,6 @@
     for jj in range(2):
         gi_x[jj] = product(2 * (1 - sec) + jj)
         go(acrosses[jj])
-    go_steps[2]()
     for jj in range(2):
         gi_h[jj] = product(2 * sec + jj)
     for jj in range(2):
@@ -538,6 +562,7 @@
     for d in range(2):
         merge_b(d, 0, d)
         go_b(d, 1, d)
+    go_steps[2]()
     for turn in range(2):
         for d in range(2):
             half = d if turn else 1 - d
@@ -591,16 +616,16 @@
         V((NZ, ROWS, WIDTH), BF16), V((NY, ROWS, WIDTH), BF16), V((NY, ROWS, WIDTH), BF16),
         V((WIDTH, NY * ROWS), BF16), V((NY, ROWS, HD), BF16), V((ROWS, WIDTH), BF16),
         V((CAP, FF), BF16), V((FF, ENC_D), BF16), V((CAP, CH), BF16),
-        V((WIDTH, PROJ), BF16), V((PROJ, CH), BF16),
+        V((WIDTH, PROJ), BF16), V((NX, PROJ, CH), BF16),
         V((NZ, 2, HALF, HD), BF16), V((NZ, 2, 8, HD), F32),
         V((2, 4, 2, HALF, HD), BF16), V((2, 4, 2, 8, HD), F32),
         V((NX, CAP, CH), BF16), V((NX, CAP, CH), BF16), V((CAP, CH), F32),
         V((8, CAP), F32), V((NX, 8, CAP), F32),
         V((NY, NZ, 8, CH), F32), V((NY, NZ, 8, CH), F32), V((NZ, 32, CH), BF16), V((NZ, 32, CH), BF16),
-        V((ROWS, CH), F32),
-        V((ROWS, WIDTH), BF16), V((2, NX, ROWS, PART), BF16), V((2, NX, ROWS, PART), BF16),
-        V((ROWS, PART), F32), V((NX, ROWS, PART), BF16), V((ROWS, CH), F32),
-        V((8, ROWS), F32), V((NX, 8, ROWS), F32), V((ROWS, CH), BF16), V((NX, ROWS, PART), BF16),
+        V((NX, 32, CH), BF16), V((NX, 32, CH), BF16),
+        V((ROWS, WIDTH), BF16), V((NX, 32, PROJ), BF16), V((NX, 32, PROJ), BF16), V((32, PROJ), F32),
+        V((NX, 32, PROJ), BF16), V((NX, 32, CH), F32), V((NX, 32, CH), BF16), V((NX, 32, CH), BF16),
+        V((NX, 32, HD), F32), V((NX, 32, PROJ), BF16), V((ROWS, ROWS), F32),
         V((2, HD, HD), F32),
     ]
     scratch += [
@@ -613,7 +638,7 @@
     scratch += [
         D((9,)), D((2, 4, 2)), D((2, 4, 2)), D((6,)), D((6,)),
         D((2, 4, 2)), D((2, 4, 2)), D((2, 4, 2)), D((2, 4, 2)),
-        D((7, 3)), D((7, 3)), D((3,)), D((3,)), D((7,)), D((7,)),
+        D((10, 3)), D((10, 3)), D((3,)), D((3,)), D((3,)), D((3,)), D((7,)), D((7,)),
         D((2, 2)), D((2, 2)), D((3, 3)), D((3, 3)), D((2, 7)), D((2, 7)), D((2, 4, 2)), D((2, 4, 2)),
     ]
     aligned, grad_in_t, grad_out = pl.pallas_call(

time: 124 us -> 135 us (1.089)
  Pallas kernels: 123 us -> 134 us
    pallas_call x1, Pallas kernels: 121 us -> 132 us  [body(): pl.pallas_call(kernel, out_shape=(jax.ShapeDtypeStruct((1, ROWS), F32), j...]
where the time goes in v3:
time: 135 us; the launch traced here: 134 us
  Pallas kernels  134 us (99%)
    pallas_call x1, Pallas kernels, body(): pl.pallas_call(kernel, out_shape=(jax.ShapeDtypeStruct((1, ROWS), F32), j...  132 us

profile of v3, /device:TPU:1, one launch (start us, length us, event | category | flops | bytes accessed | tf_op | source)
XLA Modules:
  0.0 134.5 jit_solution(8273339053144518308)
XLA Ops:
  0.6 132.3 %align.1 = (f32[1,128]{1,0:T(1,128)}, f32[32,768]{1,0:T(8,128)}, f32[32,384]{1,0:T(8,128)}) custom-call(bf16[128,768]{1,0:T(8,128)(2,1)} %q_hbm.1, bf16[128,768]{1,0:T(8,128)(2,1)} %k_hbm.1, bf16[128,768]{1,0:T(8,128)(2,1)} %v_hbm.1, bf16[128,768]{1,0:T(8,128)(2,1)} %res_hbm.1, s32[1,4096]{1,0:T(1,128)} %seg_ref.1, s32[1,32]{1,0:T(1,128)} %cnt_ref.1, ...), custom_call_target="tpu_custom_call" | custom-call | tf_op jit(solution)/shard_map/align/pallas_call | solution.py:644
  132.9 1.6 %hand_on.1 = (f32[1,128]{1,0:T(1,128)}, f32[32,768]{1,0:T(8,128)}, f32[32,384]{1,0:T(8,128)}) custom-call(f32[1,128]{1,0:T(1,128)} %get-tuple-element.9.a, f32[32,768]{1,0:T(8,128)} %get-tuple-element.10.b, f32[32,384]{1,0:T(8,128)} %get-tuple-element.11.c), custom_call_target="tpu_custom_call" | custom-call | tf_op jit(solution)/shard_map/hand_on/pallas_call | solution.py:669

commit v4 on v3

--- a/solution.py
+++ b/solution.py
@@ -47,11 +47,10 @@
     qbuf, kbuf, vbuf, vt, ko, resv, ehv, edv, erv, pin, pfull,
     opart, stats, oin, sin,
     esend, erecv, share, estat, estat_in, packed, arecv, aturn, alast, tsend, tgt,
-    hidden, fpart, frecv, first, actall, second, bsend, backall, alall, dall, column_weight, segrow,
-    go_x, go_xr, go_h, go_yr, go_z, go_zr,
-    gi_x, gi_xr, gi_h, a_y, a_yr, a_z, a_zr, b_z, b_in, b_y, b_yr,
+    hgrp, fpart, frecv, first, act_rows, second, bsend, bgrp, alall, column_weight,
+    apiece, agrp, dpiece, dgrp, gz, gz_in, segrow,
     lsem, q_s, q_r, kv_s, kv_r, o_s, o_r, os_s, os_r, x_s, x_r, pc_s, pc_r, ay_s, ay_r, az_s, az_r,
-    gx_s, gx_r, gy_s, gy_r, gz_s, gz_r, gb_s, gb_r,
+    gx_s, gx_r, gy_s, gy_r, gz_s, gz_r, gg_s, gg_r,
 ):
     sec = lax.axis_index("section")
     seq = lax.axis_index("seq")
@@ -86,7 +85,7 @@
     greeted = [{"seq": y * NZ + lax.rem(z + r, NZ)} for r in range(1, NZ)]
     greeted += [{"seq": lax.rem(y + r, NY) * NZ + z} for r in range(1, NY)]
     greeted += [{"mp": lax.rem(x + r, NX)} for r in range(1, NX)]
-    greeted += [{"section": 1 - sec}]
+    greeted += [{"section": 1 - sec, "seq": lax.rem(y + r, NY) * NZ + z} for r in range(NY)]
     for device in greeted:
         pl.semaphore_signal(barrier, inc=1, device_id=device, device_id_type=MESH)
     pl.semaphore_wait(barrier, len(greeted))
@@ -124,6 +123,36 @@
                      {"mp": lax.rem(x + r, NX)})
             for r in (1, 2, 3)
         }
+
+    def y_copies(n, ref_of):
+        return {
+            r: rcopy(ref_of(), ref_of(), gy_s.at[n, r - 1], gy_r.at[n, NY - r - 1],
+                     {"seq": lax.rem(y + r, NY) * NZ + z})
+            for r in (1, 2, 3)
+        }
+
+    def core_copy(n, ref):
+        return rcopy(ref, ref, gx_s.at[n], gx_r.at[n], {"section": 1 - sec})
+
+    def group_copies(n, pieces, group):
+        copies = []
+        for ds in range(2):
+            for r in range(NY):
+                if ds or r:
+                    to_sec, to_y = lax.rem(sec + ds, 2), lax.rem(y + r, NY)
+                    copies.append(rcopy(
+                        pieces.at[to_sec, to_y], group.at[x, sec, y],
+                        gg_s.at[n, ds * NY + r], gg_r.at[n, ds * NY + (NY - r) % NY],
+                        {"section": to_sec, "seq": to_y * NZ + z}))
+        return copies
+
+    def send_pieces(copies, rows, pieces, group):
+        for a in range(2):
+            for b in range(NY):
+                pieces[a, b] = rows[:, (a * NY + b) * 256:(a * NY + b + 1) * 256]
+        for copy in copies:
+            go(copy)
+        group[x, sec, y] = pieces[sec, y]
 
     local[3].wait()
     local[4].wait()
@@ -300,9 +329,6 @@
     for d in range(2):
         go_o(d, 1, 1 - d)
     send_rows()
-    for r in (1, 3, 2):
-        take(p_copies[NX - r])
-        go(pc_copies[r])
     attend_two(2)
 
     def merge(r, d, t, half):
@@ -341,19 +367,26 @@
             merge(0, d, 3, half)
     for r in (4, 3, 5, 2, 6, 1, 7):
         go(row_zs[r])
+    for r in (1, 3, 2):
+        take(p_copies[NX - r])
+        go(pc_copies[r])
     local[6].wait()
     for h in range(HEADS):
         half, i = h // 3, h % 3
         cols = slice(h * HD, (h + 1) * HD)
         attn = opart[0, half, i * HD:(i + 1) * HD].astype(F32) / stats[0, half, 3 + i:4 + i]
         attn = attn.T.astype(BF16).astype(F32)
-        hidden[:, cols] = (resv[:, cols].astype(F32) + attn).astype(BF16)
-
+        hgrp[sec, y, :, cols] = (resv[:, cols].astype(F32) + attn).astype(BF16)
+
+    h_copies = y_copies(0, lambda: hgrp.at[sec, y])
+    for r in (2, 1, 3):
+        go(h_copies[r])
     local[7].wait()
+    hidden = hgrp[sec, y]
     f_copies = []
     for c in range(2):
         cols = slice(c * 1024, (c + 1) * 1024)
-        fpart[:, :, cols] = dot(hidden[...], pin[:, cols]).astype(BF16).reshape(NX, 32, 1024)
+        fpart[:, :, cols] = dot(hidden, pin[:, cols]).astype(BF16).reshape(NX, 32, 1024)
         f_copies.append(x_copies(
             2 + c, lambda r: fpart.at[lax.rem(x + r, NX), :, cols], lambda r: frecv.at[r, :, cols]))
         for r in (2, 1, 3):
@@ -385,11 +418,10 @@
         for r in (1, 2, 3):
             value = value + frecv[r, :, cols].astype(F32)
         first[:, cols] = value
-        actall[x, :, cols] = (value * jax.nn.sigmoid(value)).astype(BF16)
-    act_copies = x_copies(4, lambda r: actall.at[x], lambda r: actall.at[x])
-    for r in (2, 1, 3):
-        go(act_copies[r])
-    act = actall[x]
+        act_rows[:, cols] = (value * jax.nn.sigmoid(value)).astype(BF16)
+    act = act_rows[...]
+    act_pieces = group_copies(0, apiece, agrp)
+    send_pieces(act_pieces, act, apiece, agrp)
     for r in range(NX):
         if r:
             take(pc_copies[r])
@@ -408,198 +440,90 @@
     weight = column_weight[pl.ds(pl.multiple_of(x * 32, 32), 32), 0:1]
     by_target = -weight / (norm_z * norm_f)
     by_second = weight * aligned / (norm_z * norm_z)
-    b_copies = x_copies(6, lambda r: bsend.at[r], lambda r: backall.at[x])
+    b_copies = x_copies(6, lambda r: bsend.at[r], lambda r: bgrp.at[sec, y, x])
     for r in (2, 1, 3, 0):
         bsend[r] = (by_target * tgt[r].astype(F32) + by_second * second[r]).astype(BF16)
         if r:
             go(b_copies[r])
-    backall[x] = bsend[0]
+    bgrp[sec, y, x] = bsend[0]
     alall[x] = jnp.broadcast_to(aligned, (32, HD))
     l_copies = x_copies(7, lambda r: alall.at[x], lambda r: alall.at[x])
     for r in (2, 1, 3):
         go(l_copies[r])
+    for copy in act_pieces:
+        take(copy)
+    act_copies = x_copies(4, lambda r: agrp.at[x], lambda r: agrp.at[x])
+    for r in (2, 1, 3):
+        go(act_copies[r])
     upstream = dot(bsend[0], pfull[0], 1, 1)
     for r in (1, 2, 3):
         upstream = upstream + dot(bsend[r], pfull[r], 1, 1)
     value = first[...]
     sig = jax.nn.sigmoid(value)
-    dall[x] = (upstream * sig * (1.0 + value * (1.0 - sig))).astype(BF16)
-    d_copies = x_copies(8, lambda r: dall.at[x], lambda r: dall.at[x])
+    dfirst = (upstream * sig * (1.0 + value * (1.0 - sig))).astype(BF16)
+    d_pieces = group_copies(1, dpiece, dgrp)
+    send_pieces(d_pieces, dfirst, dpiece, dgrp)
+    for r in (1, 2, 3):
+        take(b_copies[NX - r])
+    back_copies = y_copies(1, lambda: bgrp.at[sec, y])
+    for r in (2, 1, 3):
+        go(back_copies[r])
+    for r in (1, 2, 3):
+        take(h_copies[NY - r])
+    hidden_core = core_copy(0, hgrp.at[sec])
+    go(hidden_core)
+    for copy in d_pieces:
+        take(copy)
+    d_copies = x_copies(8, lambda r: dgrp.at[x], lambda r: dgrp.at[x])
     for r in (2, 1, 3):
         go(d_copies[r])
     for r in (1, 2, 3):
-        take(act_copies[NX - r])
-        take(b_copies[NX - r])
         take(l_copies[NX - r])
     al_ref[...] = alall[...].reshape(ROWS, HD).T[0:1]
-
-    def reduction(n, left, right, xs, xr, hs, yr, zs, zr, out):
-        def across(jj):
-            return rcopy(xs.at[jj], xr.at[jj], gx_s.at[n, jj], gx_r.at[n, jj], {"section": 1 - sec})
-
-        def y_copy(r):
-            peer = lax.rem(y + r, NY)
-            return rcopy(hs.at[peer], yr.at[NY - r], gy_s.at[n, r - 1], gy_r.at[n, NY - r - 1],
-                         {"seq": peer * NZ + z})
-
-        def z_copy(r):
+    for r in (1, 2, 3):
+        take(back_copies[NY - r])
+    back_core = core_copy(1, bgrp.at[sec])
+    go(back_core)
+    for r in (1, 2, 3):
+        take(act_copies[NX - r])
+    take(back_core)
+
+    def z_copies(n):
+        copies = {}
+        for r in range(1, NZ):
             peer = lax.rem(z + r, NZ)
-            return rcopy(zs.at[peer], zr.at[NZ - r], gz_s.at[n, r - 1], gz_r.at[n, NZ - r - 1],
-                         {"seq": y * NZ + peer})
-
-        acrosses = [across(jj) for jj in range(2)]
-        y_copies = {r: y_copy(r) for r in range(1, NY)}
-        z_copies = {r: z_copy(r) for r in range(1, NZ)}
-
-        def product(j):
-            cols = pl.ds(pl.multiple_of(j * PART, PART), PART)
-            return dot(left[:, :, cols].reshape(ROWS, PART), right[...].reshape(ROWS, -1), 0, 0).astype(BF16)
-
-        def start():
-            for jj in range(2):
-                xs[jj] = product(2 * (1 - sec) + jj)
-                go(acrosses[jj])
-            for jj in range(2):
-                value = product(2 * sec + jj)
-                for b in range(2):
-                    hs[2 * jj + b] = value[b * 256:(b + 1) * 256]
-
-        def middle():
-            for jj in range(2):
-                take(acrosses[jj])
-                for b in range(2):
-                    hs[2 * jj + b] = (hs[2 * jj + b].astype(F32)
-                                      + xr[jj, b * 256:(b + 1) * 256].astype(F32)).astype(BF16)
-            for r in (2, 1, 3):
-                go(y_copies[r])
-
-        def late():
-            for r in (1, 2, 3):
-                take(y_copies[NY - r])
-            value = hs[y].astype(F32)
-            for r in (1, 2, 3):
-                value = value + yr[r].astype(F32)
-            zs[...] = value.astype(BF16).reshape(zs.shape)
-            for r in (4, 3, 5, 2, 6, 1, 7):
-                go(z_copies[r])
-
-        def end():
-            for r in range(1, NZ):
-                take(z_copies[NZ - r])
-            value = zs[z].astype(F32)
-            for r in range(1, NZ):
-                value = value + zr[r].astype(F32)
-            out[...] = value
-
-        return start, middle, late, end
-
-    go_steps = reduction(0, actall, backall, go_x, go_xr, go_h, go_yr, go_z, go_zr, go_ref)
-    go_steps[0]()
-
-    go_steps[1]()
+            copies[r] = rcopy(gz.at[n, peer], gz_in.at[n, NZ - r], gz_s.at[n, r - 1], gz_r.at[n, NZ - r - 1],
+                              {"seq": y * NZ + peer})
+        return copies
+
+    z_all = [z_copies(n) for n in range(3)]
+
+    def product(n, left, right_of):
+        value = 0.0
+        for b in range(NX):
+            rows = left[b].reshape(CAP, CAP)
+            value = value + dot(rows, right_of(b).reshape(CAP, CH), 0, 0)
+        gz[n] = value.astype(BF16).reshape(NZ, 32, CH)
+        for r in (4, 3, 5, 2, 6, 1, 7):
+            go(z_all[n][r])
+
+    def finish(n):
+        for r in range(1, NZ):
+            take(z_all[n][NZ - r])
+        value = gz[n, z].astype(F32)
+        for r in range(1, NZ):
+            value = value + gz_in[n, r].astype(F32)
+        return value
+
+    product(0, agrp, lambda b: bgrp[:, :, b])
+    take(hidden_core)
     for r in (1, 2, 3):
         take(d_copies[NX - r])
-
-    def across(jj):
-        return rcopy(gi_x.at[jj], gi_xr.at[jj], gx_s.at[1, jj], gx_r.at[1, jj], {"section": 1 - sec})
-
-    def product(j):
-        cols = pl.ds(pl.multiple_of(j * PART, PART), PART)
-        return dot(dall[:, :, cols].reshape(ROWS, PART), hidden[...], 0, 0).astype(BF16)
-
-    def ya_copy(r):
-        peer = lax.rem(y + r, NY)
-        return rcopy(a_y.at[peer], a_yr.at[NY - r], gy_s.at[1, r - 1], gy_r.at[1, NY - r - 1], {"seq": peer * NZ + z})
-
-    def za_copy(r):
-        peer = lax.rem(z + r, NZ)
-        return rcopy(a_z.at[peer], a_zr.at[NZ - r], gz_s.at[1, r - 1], gz_r.at[1, NZ - r - 1], {"seq": y * NZ + peer})
-
-    def yb_copy(r):
-        peer = lax.rem(y + r, NY)
-        return rcopy(b_y.at[peer], b_yr.at[NY - r], gy_s.at[2, r - 1], gy_r.at[2, NY - r - 1], {"seq": peer * NZ + z})
-
-    def zb_copy(d, t, half):
-        chunk = lax.rem(z + (4 - t if d == 0 else 4 + t), NZ)
-        part = pl.ds(2 * half, 2)
-        return rcopy(b_z.at[chunk, part], b_in.at[d, t, part], gb_s.at[d, t, half], gb_r.at[d, t, half],
-                     zp if d == 0 else zm)
-
-    acrosses = [across(jj) for jj in range(2)]
-    ya_copies = {r: ya_copy(r) for r in range(1, NY)}
-    za_copies = {r: za_copy(r) for r in range(1, NZ)}
-    yb_copies = {r: yb_copy(r) for r in range(1, NY)}
-    zb_copies = [[{h: zb_copy(d, t, h) for h in ((0, 1) if t else (d,))} for t in range(4)] for d in range(2)]
-    for jj in range(2):
-        gi_x[jj] = product(2 * (1 - sec) + jj)
-        go(acrosses[jj])
-    for jj in range(2):
-        gi_h[jj] = product(2 * sec + jj)
-    for jj in range(2):
-        take(acrosses[jj])
-        for b in range(2):
-            rows = slice(b * 256, (b + 1) * 256)
-            value = (gi_h[jj, rows].astype(F32) + gi_xr[jj, rows].astype(F32)).astype(BF16)
-            a_y[2 * jj + b] = value[:, 0:HALF]
-            for n in range(NZ):
-                b_z[n, 2 * jj + b] = value[n * 32:(n + 1) * 32, HALF:WIDTH]
-
-    def go_b(d, t, half):
-        go(zb_copies[d][t][half])
-
-    def merge_b(d, t, half):
-        take(zb_copies[d][t][half])
-        chunk = lax.rem(z + (3 - t if d == 0 else 5 + t), NZ)
-        part = pl.ds(2 * half, 2)
-        b_z[chunk, part] = (b_z[chunk, part].astype(F32) + b_in[d, t, part].astype(F32)).astype(BF16)
-
-    for d in range(2):
-        go_b(d, 0, d)
-    for r in (2, 1, 3):
-        go(ya_copies[r])
-    for d in range(2):
-        go_b(d, 1, 1 - d)
-    for d in range(2):
-        merge_b(d, 0, d)
-        go_b(d, 1, d)
-    go_steps[2]()
-    for turn in range(2):
-        for d in range(2):
-            half = d if turn else 1 - d
-            merge_b(d, 1, half)
-            go_b(d, 2, half)
-    for r in (1, 2, 3):
-        take(ya_copies[NY - r])
-    value = a_y[y].astype(F32)
-    for r in (1, 2, 3):
-        value = value + a_yr[r].astype(F32)
-    a_z[...] = value.astype(BF16).reshape(NZ, 32, HALF)
-    for r in (4, 3, 5, 2, 6, 1, 7):
-        go(za_copies[r])
-    for turn in range(2):
-        for d in range(2):
-            half = d if turn else 1 - d
-            merge_b(d, 2, half)
-            go_b(d, 3, half)
-    for half in range(2):
-        for d in range(2):
-            merge_b(d, 3, half)
-    b_y[...] = b_z[z]
-    for r in (2, 1, 3):
-        go(yb_copies[r])
-    go_steps[3]()
-    for r in range(1, NZ):
-        take(za_copies[NZ - r])
-    value = a_z[z].astype(F32)
-    for r in range(1, NZ):
-        value = value + a_zr[r].astype(F32)
-    gi_ref[:, 0:HALF] = value
-    for r in (1, 2, 3):
-        take(yb_copies[NY - r])
-    value = b_y[y].astype(F32)
-    for r in (1, 2, 3):
-        value = value + b_yr[r].astype(F32)
-    gi_ref[:, HALF:WIDTH] = value
+    for n in range(2):
+        product(1 + n, dgrp, lambda b: hgrp[:, :, b * 32:(b + 1) * 32, n * CH:(n + 1) * CH])
+    go_ref[...] = finish(0)
+    for n in range(2):
+        gi_ref[:, n * CH:(n + 1) * CH] = finish(1 + n)
 
     for copy in pending:
         copy.wait_send()
@@ -623,23 +547,19 @@
         V((8, CAP), F32), V((NX, 8, CAP), F32),
         V((NY, NZ, 8, CH), F32), V((NY, NZ, 8, CH), F32), V((NZ, 32, CH), BF16), V((NZ, 32, CH), BF16),
         V((NX, 32, CH), BF16), V((NX, 32, CH), BF16),
-        V((ROWS, WIDTH), BF16), V((NX, 32, PROJ), BF16), V((NX, 32, PROJ), BF16), V((32, PROJ), F32),
-        V((NX, 32, PROJ), BF16), V((NX, 32, CH), F32), V((NX, 32, CH), BF16), V((NX, 32, CH), BF16),
-        V((NX, 32, HD), F32), V((NX, 32, PROJ), BF16), V((ROWS, ROWS), F32),
+        V((2, NY, ROWS, WIDTH), BF16), V((NX, 32, PROJ), BF16), V((NX, 32, PROJ), BF16), V((32, PROJ), F32),
+        V((32, PROJ), BF16), V((NX, 32, CH), F32), V((NX, 32, CH), BF16), V((2, NY, NX, 32, CH), BF16),
+        V((NX, 32, HD), F32), V((ROWS, ROWS), F32),
+        V((2, NY, 32, 256), BF16), V((NX, 2, NY, 32, 256), BF16),
+        V((2, NY, 32, 256), BF16), V((NX, 2, NY, 32, 256), BF16),
+        V((3, NZ, 32, CH), BF16), V((3, NZ, 32, CH), BF16),
         V((2, HD, HD), F32),
-    ]
-    scratch += [
-        V((2, PART, CH), BF16), V((2, PART, CH), BF16), V((NY, 256, CH), BF16),
-        V((NY, 256, CH), BF16), V((NZ, 32, CH), BF16), V((NZ, 32, CH), BF16),
-        V((2, PART, WIDTH), BF16), V((2, PART, WIDTH), BF16), V((2, PART, WIDTH), BF16),
-        V((NY, 256, HALF), BF16), V((NY, 256, HALF), BF16), V((NZ, 32, HALF), BF16), V((NZ, 32, HALF), BF16),
-        V((NZ, NY, 32, HALF), BF16), V((2, 4, NY, 32, HALF), BF16), V((NY, 32, HALF), BF16), V((NY, 32, HALF), BF16),
     ]
     scratch += [
         D((9,)), D((2, 4, 2)), D((2, 4, 2)), D((6,)), D((6,)),
         D((2, 4, 2)), D((2, 4, 2)), D((2, 4, 2)), D((2, 4, 2)),
         D((10, 3)), D((10, 3)), D((3,)), D((3,)), D((3,)), D((3,)), D((7,)), D((7,)),
-        D((2, 2)), D((2, 2)), D((3, 3)), D((3, 3)), D((2, 7)), D((2, 7)), D((2, 4, 2)), D((2, 4, 2)),
+        D((2,)), D((2,)), D((2, 3)), D((2, 3)), D((3, 7)), D((3, 7)), D((2, 8)), D((2, 8)),
     ]
     aligned, grad_in_t, grad_out = pl.pallas_call(
         kernel,

time: 135 us -> 121 us (0.90)
  Pallas kernels: 134 us -> 120 us
    pallas_call x1, Pallas kernels: 132 us -> 119 us  [body(): pl.pallas_call(kernel, out_shape=(jax.ShapeDtypeStruct((1, ROWS), F32), j...]
where the time goes in v4:
time: 121 us
  Pallas kernels  120 us (99%)
    pallas_call x1, Pallas kernels, body(): pl.pallas_call(kernel, out_shape=(jax.ShapeDtypeStruct((1, ROWS), F32), j...  119 us

profile of v4, /device:TPU:1, one launch (start us, length us, event | category | flops | bytes accessed | tf_op | source)
XLA Modules:
  0.0 120.8 jit_solution(9499859090340485237)
XLA Ops:
  0.6 118.6 %align.1 = (f32[1,128]{1,0:T(1,128)}, f32[32,768]{1,0:T(8,128)}, f32[32,384]{1,0:T(8,128)}) custom-call(bf16[128,768]{1,0:T(8,128)(2,1)} %q_hbm.1, bf16[128,768]{1,0:T(8,128)(2,1)} %k_hbm.1, bf16[128,768]{1,0:T(8,128)(2,1)} %v_hbm.1, bf16[128,768]{1,0:T(8,128)(2,1)} %res_hbm.1, s32[1,4096]{1,0:T(1,128)} %seg_ref.1, s32[1,32]{1,0:T(1,128)} %cnt_ref.1, ...), custom_call_target="tpu_custom_call" | custom-call | tf_op jit(solution)/shard_map/align/pallas_call | solution.py:564
  119.2 1.6 %hand_on.1 = (f32[1,128]{1,0:T(1,128)}, f32[32,768]{1,0:T(8,128)}, f32[32,384]{1,0:T(8,128)}) custom-call(f32[1,128]{1,0:T(1,128)} %get-tuple-element.9.a, f32[32,768]{1,0:T(8,128)} %get-tuple-element.10.b, f32[32,384]{1,0:T(8,128)} %get-tuple-element.11.c), custom_call_target="tpu_custom_call" | custom-call | tf_op jit(solution)/shard_map/hand_on/pallas_call | solution.py:589

commit v5 on v4

--- a/solution.py
+++ b/solution.py
@@ -49,7 +49,7 @@
     esend, erecv, share, estat, estat_in, packed, arecv, aturn, alast, tsend, tgt,
     hgrp, fpart, frecv, first, act_rows, second, bsend, bgrp, alall, column_weight,
     apiece, agrp, dpiece, dgrp, gz, gz_in, segrow,
-    lsem, q_s, q_r, kv_s, kv_r, o_s, o_r, os_s, os_r, x_s, x_r, pc_s, pc_r, ay_s, ay_r, az_s, az_r,
+    lsem, q_s, q_r, kv_s, kv_r, o_s, o_r, os_s, os_r, x_s, x_r, pc_s, pc_r, pr_s, pr_r, ay_s, ay_r, az_s, az_r,
     gx_s, gx_r, gy_s, gy_r, gz_s, gz_r, gg_s, gg_r,
 ):
     sec = lax.axis_index("section")
@@ -77,8 +77,13 @@
         (er_hbm, erv), (res_hbm, resv), (pin_hbm, pin), (pout_hbm, pfull.at[0]),
     )):
         copy = pltpu.make_async_copy(src, dst, lsem.at[n])
-        copy.start()
         local.append(copy)
+
+    def fetch(first, last):
+        for n in range(first, last):
+            local[n].start()
+
+    fetch(0, 3)
 
     barrier = pltpu.get_barrier_semaphore()
 
@@ -106,22 +111,22 @@
 
     q_copies = [[{h: q_copy(d, t, h) for h in ((0, 1) if t < 3 else (d,))} for t in range(4)] for d in range(2)]
     kv_copies = [kv_copy(n) for n in range(6)]
-    local[0].wait()
+    for n in range(3):
+        local[n].wait()
+    fetch(3, 9)
     for half in range(2):
         for d in range(2):
             go(q_copies[d][0][half])
-    local[1].wait()
     go(kv_copies[0])
     go(kv_copies[1])
-    local[2].wait()
     go(kv_copies[2])
     go(kv_copies[3])
 
-    def x_copies(phase, src_of, dst_of):
+    def x_copies(phase, src_of, dst_of, which=(1, 2, 3)):
         return {
             r: rcopy(src_of(r), dst_of(NX - r), x_s.at[phase, r - 1], x_r.at[phase, NX - r - 1],
                      {"mp": lax.rem(x + r, NX)})
-            for r in (1, 2, 3)
+            for r in which
         }
 
     def y_copies(n, ref_of):
@@ -163,13 +168,17 @@
         if r:
             go(enc_copies[r])
 
-    local[8].wait()
     core_rows = pl.ds(pl.multiple_of(sec * (PROJ // 2), PROJ // 2), PROJ // 2)
-    p_copies = x_copies(9, lambda r: pfull.at[0, core_rows], lambda r: pfull.at[r, core_rows])
+    p_copies = x_copies(9, lambda r: pfull.at[0, core_rows], lambda r: pfull.at[r, core_rows], (1, 3))
+
+    def relay(n):
+        part = pl.ds(pl.multiple_of(sec * (PROJ // 2) + n * PART, PART), PART)
+        return rcopy(pfull.at[(3, 1)[n], part], pfull.at[2, part], pr_s.at[n], pr_r.at[n],
+                     {"mp": lax.rem(x + (1, 3)[n], NX)})
+
+    relays = [relay(0), relay(1)]
     pc_copies = {r: rcopy(pfull.at[r, core_rows], pfull.at[r, core_rows], pc_s.at[r - 1], pc_r.at[r - 1],
                           {"section": 1 - sec}) for r in (1, 2, 3)}
-    for r in (1, 3, 2):
-        go(p_copies[r])
     ids = iota((16, NSEQ * ROWS), 0)
     seg = seg_ref[...]
     below = jnp.sum(jnp.where(seg < ids, 1.0, 0.0), axis=1, keepdims=True)
@@ -229,6 +238,16 @@
             estat[:, b * HD:(b + 1) * HD] = packed_stat[b * HD:(b + 1) * HD].T[0:8]
         for r in (2, 1, 3):
             go(stat_copies[r])
+
+    def gather_out():
+        local[8].wait()
+        for r in (1, 3):
+            go(p_copies[r])
+
+    def relay_out():
+        for n in range(2):
+            take(p_copies[(1, 3)[n]])
+            go(relays[n])
 
 
     def send_rows():
@@ -258,30 +277,35 @@
             go(row_ys[r])
         arecv[pl.ds(y, 1)] = packed[pl.ds(y, 1)]
 
-    def attend(r):
-        device = y * NZ + lax.rem(z + r, NZ)
-        image = jnp.where(image_columns(device), 1.0, 0.0).astype(BF16)
+    def attend(pair):
         keys_image = ko[...].reshape(NY * ROWS, HD)
-        for h in range(HEADS):
-            cols = slice(h * HD, (h + 1) * HD)
-            keys = jnp.concatenate([kbuf[:, :, cols].reshape(NY * ROWS, HD), keys_image], axis=1)
-            scores = dot(keys, jnp.concatenate([qbuf[r, :, cols], image], axis=1), 1, 1)
-            best = jnp.max(scores, axis=0, keepdims=True)
-            prob = jnp.exp2((scores - best) * EXP_SCALE)
-            half, i = h // 3, h % 3
-            stats[r, half, i:i + 1] = best * EXP_SCALE
-            stats[r, half, 3 + i:4 + i] = jnp.sum(prob, axis=0, keepdims=True)
-            opart[r, half, i * HD:(i + 1) * HD] = dot(vt[cols], prob.astype(BF16)).astype(BF16)
-
-    def attend_two(k):
-        def one(i, c):
-            attend(4 + k * (1 - 2 * i))
-            return c
-
-        lax.fori_loop(0, 2, one, 0)
-
-    def attend_one(r):
-        lax.fori_loop(r, r + 1, lambda i, c: (attend(i), c)[1], 0)
+        image = jnp.concatenate(
+            [jnp.where(image_columns(y * NZ + lax.rem(z + r, NZ)), 1.0, 0.0).astype(BF16) for r in pair], axis=0)
+        scores, probs = {}, {}
+        for step in range(HEADS + 2):
+            if step < HEADS:
+                cols = slice(step * HD, (step + 1) * HD)
+                keys = jnp.concatenate([kbuf[:, :, cols].reshape(NY * ROWS, HD), keys_image], axis=1)
+                rows = jnp.concatenate([qbuf[r, :, cols] for r in pair], axis=0)
+                scores[step] = dot(keys, jnp.concatenate([rows, image], axis=1), 1, 1)
+            if 1 <= step <= HEADS:
+                h = step - 1
+                score = scores.pop(h)
+                best = jnp.max(score, axis=0, keepdims=True)
+                prob = jnp.exp2((score - best) * EXP_SCALE)
+                total = jnp.sum(prob, axis=0, keepdims=True)
+                half, i = h // 3, h % 3
+                for n, r in enumerate(pair):
+                    cut = slice(n * ROWS, (n + 1) * ROWS)
+                    stats[r, half, i:i + 1] = best[:, cut] * EXP_SCALE
+                    stats[r, half, 3 + i:4 + i] = total[:, cut]
+                probs[h] = prob.astype(BF16)
+            if step >= 2:
+                h = step - 2
+                half, i = h // 3, h % 3
+                mixed = dot(vt[h * HD:(h + 1) * HD], probs.pop(h)).astype(BF16)
+                for n, r in enumerate(pair):
+                    opart[r, half, i * HD:(i + 1) * HD] = mixed[:, n * ROWS:(n + 1) * ROWS]
 
     def turn_values(r):
         vt[:, r * ROWS:(r + 1) * ROWS] = vbuf[r].T
@@ -304,32 +328,33 @@
 
     forward_q(0, 0)
     forward_q(0, 1)
+    forward_q(1, 0)
     take(kv_copies[0])
     go(kv_copies[4])
-    take(kv_copies[1])
-    forward_q(1, 0)
-    take(kv_copies[2])
+    forward_q(1, 1)
     take(kv_copies[3])
     go(kv_copies[5])
-    forward_q(1, 1)
+    take(kv_copies[1])
+    take(kv_copies[2])
     for r in (0, 1, 3):
         turn_values(r)
     forward_q(2, 0)
     sum_encoder()
+    gather_out()
     forward_q(2, 1)
     for n in (4, 5):
         take(kv_copies[n])
     turn_values(2)
-    attend_two(1)
+    attend((5, 3))
     forward_q(3, 0)
     forward_q(3, 1)
-    attend_one(4)
+    attend((4, 0))
     for d in range(2):
         go_o(d, 0, d)
     for d in range(2):
         go_o(d, 1, 1 - d)
     send_rows()
-    attend_two(2)
+    attend((6, 2))
 
     def merge(r, d, t, half):
         mine, other = stats[r, half], sin[d, t, half]
@@ -345,9 +370,7 @@
 
     for t in (1, 2, 3):
         if t == 2:
-            attend_two(3)
-        if t == 3:
-            attend_one(0)
+            attend((7, 1))
         for turn in range(2):
             for d in range(2):
                 half = d if turn else 1 - d
@@ -356,20 +379,23 @@
                 take_o(d, t - 1, half)
                 merge(4 - t if d == 0 else 4 + t, d, t - 1, half)
                 go_o(d, t, half)
+    relay_out()
     for r in (1, 2, 3):
         take(row_ys[NY - r])
     for n in range(NZ):
         aturn[n] = arecv[:, n].reshape(NY * 8, CH).astype(BF16)
     alast[pl.ds(z, 1)] = aturn[pl.ds(z, 1)]
+    for r in (4, 3, 5, 2, 6, 1, 7):
+        go(row_zs[r])
     for half in range(2):
         for d in range(2):
             take_o(d, 3, half)
             merge(0, d, 3, half)
-    for r in (4, 3, 5, 2, 6, 1, 7):
-        go(row_zs[r])
-    for r in (1, 3, 2):
-        take(p_copies[NX - r])
+    for r in (1, 3):
         go(pc_copies[r])
+    for n in range(2):
+        take(relays[n])
+    go(pc_copies[2])
     local[6].wait()
     for h in range(HEADS):
         half, i = h // 3, h % 3
@@ -402,14 +428,6 @@
     place = (iota((ROWS, CAP), 0) * NSEQ + seq).astype(F32)
     chosen = jnp.where((place >= low) & (place < high), 1.0, 0.0).astype(BF16)
 
-    for r in range(1, NZ):
-        take(row_zs[NZ - r])
-    tsend[...] = dot(chosen, alast[...].reshape(CAP, CH)).astype(BF16).reshape(NX, 32, CH)
-    t_copies = x_copies(5, lambda r: tsend.at[lax.rem(x + r, NX)], lambda r: tgt.at[r])
-    for r in (2, 1, 3):
-        go(t_copies[r])
-    tgt[0] = tsend[x]
-    column_weight[...] = jnp.broadcast_to(aw_ref[...], (ROWS, ROWS)).T
     for c in range(2):
         cols = slice(c * 1024, (c + 1) * 1024)
         for r in (1, 2, 3):
@@ -425,7 +443,21 @@
     for r in range(NX):
         if r:
             take(pc_copies[r])
+        if r == 2:
+            for copy in act_pieces:
+                take(copy)
+            act_copies = x_copies(4, lambda r: agrp.at[x], lambda r: agrp.at[x])
+            for r2 in (2, 1, 3):
+                go(act_copies[r2])
         second[r] = dot(act, pfull[r])
+    for r in range(1, NZ):
+        take(row_zs[NZ - r])
+    tsend[...] = dot(chosen, alast[...].reshape(CAP, CH)).astype(BF16).reshape(NX, 32, CH)
+    t_copies = x_copies(5, lambda r: tsend.at[lax.rem(x + r, NX)], lambda r: tgt.at[r])
+    for r in (2, 1, 3):
+        go(t_copies[r])
+    tgt[0] = tsend[x]
+    column_weight[...] = jnp.broadcast_to(aw_ref[...], (ROWS, ROWS)).T
     for r in (1, 2, 3):
         take(t_copies[NX - r])
     inner = square_z = square_f = 0.0
@@ -450,11 +482,6 @@
     l_copies = x_copies(7, lambda r: alall.at[x], lambda r: alall.at[x])
     for r in (2, 1, 3):
         go(l_copies[r])
-    for copy in act_pieces:
-        take(copy)
-    act_copies = x_copies(4, lambda r: agrp.at[x], lambda r: agrp.at[x])
-    for r in (2, 1, 3):
-        go(act_copies[r])
     upstream = dot(bsend[0], pfull[0], 1, 1)
     for r in (1, 2, 3):
         upstream = upstream + dot(bsend[r], pfull[r], 1, 1)
@@ -558,7 +585,7 @@
     scratch += [
         D((9,)), D((2, 4, 2)), D((2, 4, 2)), D((6,)), D((6,)),
         D((2, 4, 2)), D((2, 4, 2)), D((2, 4, 2)), D((2, 4, 2)),
-        D((10, 3)), D((10, 3)), D((3,)), D((3,)), D((3,)), D((3,)), D((7,)), D((7,)),
+        D((10, 3)), D((10, 3)), D((3,)), D((3,)), D((2,)), D((2,)), D((3,)), D((3,)), D((7,)), D((7,)),
         D((2,)), D((2,)), D((2, 3)), D((2, 3)), D((3, 7)), D((3, 7)), D((2, 8)), D((2, 8)),
     ]
     aligned, grad_in_t, grad_out = pl.pallas_call(

time: 121 us -> 110 us (0.909)
  Pallas kernels: 120 us -> 110 us
    pallas_call x1, Pallas kernels: 119 us -> 108 us  [body(): pl.pallas_call(kernel, out_shape=(jax.ShapeDtypeStruct((1, ROWS), F32), j...]
where the time goes in v5:
time: 110 us
  Pallas kernels  110 us (100%)
    pallas_call x1, Pallas kernels, body(): pl.pallas_call(kernel, out_shape=(jax.ShapeDtypeStruct((1, ROWS), F32), j...  108 us

profile of v5, /device:TPU:1, one launch (start us, length us, event | category | flops | bytes accessed | tf_op | source)
XLA Modules:
  0.0 110.2 jit_solution(10145254113882940006)
XLA Ops:
  0.6 108.0 %align.1 = (f32[1,128]{1,0:T(1,128)}, f32[32,768]{1,0:T(8,128)}, f32[32,384]{1,0:T(8,128)}) custom-call(bf16[128,768]{1,0:T(8,128)(2,1)} %q_hbm.1, bf16[128,768]{1,0:T(8,128)(2,1)} %k_hbm.1, bf16[128,768]{1,0:T(8,128)(2,1)} %v_hbm.1, bf16[128,768]{1,0:T(8,128)(2,1)} %res_hbm.1, s32[1,4096]{1,0:T(1,128)} %seg_ref.1, s32[1,32]{1,0:T(1,128)} %cnt_ref.1, ...), custom_call_target="tpu_custom_call" | custom-call | tf_op jit(solution)/shard_map/align/pallas_call | solution.py:591
  108.6 1.6 %hand_on.1 = (f32[1,128]{1,0:T(1,128)}, f32[32,768]{1,0:T(8,128)}, f32[32,384]{1,0:T(8,128)}) custom-call(f32[1,128]{1,0:T(1,128)} %get-tuple-element.9.a, f32[32,768]{1,0:T(8,128)} %get-tuple-element.10.b, f32[32,384]{1,0:T(8,128)} %get-tuple-element.11.c), custom_call_target="tpu_custom_call" | custom-call | tf_op jit(solution)/shard_map/hand_on/pallas_call | solution.py:616

commit v6 on v5

--- a/solution.py
+++ b/solution.py
@@ -248,6 +248,7 @@
         for n in range(2):
             take(p_copies[(1, 3)[n]])
             go(relays[n])
+            go(pc_copies[(3, 1)[n]])
 
 
     def send_rows():
@@ -379,7 +380,8 @@
                 take_o(d, t - 1, half)
                 merge(4 - t if d == 0 else 4 + t, d, t - 1, half)
                 go_o(d, t, half)
-    relay_out()
+        if t == 2:
+            relay_out()
     for r in (1, 2, 3):
         take(row_ys[NY - r])
     for n in range(NZ):
@@ -391,8 +393,6 @@
         for d in range(2):
             take_o(d, 3, half)
             merge(0, d, 3, half)
-    for r in (1, 3):
-        go(pc_copies[r])
     for n in range(2):
         take(relays[n])
     go(pc_copies[2])
@@ -440,6 +440,14 @@
     act = act_rows[...]
     act_pieces = group_copies(0, apiece, agrp)
     send_pieces(act_pieces, act, apiece, agrp)
+    for r in range(1, NZ):
+        take(row_zs[NZ - r])
+    tsend[...] = dot(chosen, alast[...].reshape(CAP, CH)).astype(BF16).reshape(NX, 32, CH)
+    t_copies = x_copies(5, lambda r: tsend.at[lax.rem(x + r, NX)], lambda r: tgt.at[r])
+    for r in (2, 1, 3):
+        go(t_copies[r])
+    tgt[0] = tsend[x]
+    column_weight[...] = jnp.broadcast_to(aw_ref[...], (ROWS, ROWS)).T
     for r in range(NX):
         if r:
             take(pc_copies[r])
@@ -450,14 +458,6 @@
             for r2 in (2, 1, 3):
                 go(act_copies[r2])
         second[r] = dot(act, pfull[r])
-    for r in range(1, NZ):
-        take(row_zs[NZ - r])
-    tsend[...] = dot(chosen, alast[...].reshape(CAP, CH)).astype(BF16).reshape(NX, 32, CH)
-    t_copies = x_copies(5, lambda r: tsend.at[lax.rem(x + r, NX)], lambda r: tgt.at[r])
-    for r in (2, 1, 3):
-        go(t_copies[r])
-    tgt[0] = tsend[x]
-    column_weight[...] = jnp.broadcast_to(aw_ref[...], (ROWS, ROWS)).T
     for r in (1, 2, 3):
         take(t_copies[NX - r])
     inner = square_z = square_f = 0.0

time: 110 us -> 103 us (0.936)
  Pallas kernels: 110 us -> 102 us
    pallas_call x1, Pallas kernels: 108 us -> 100 us  [body(): pl.pallas_call(kernel, out_shape=(jax.ShapeDtypeStruct((1, ROWS), F32), j...]
where the time goes in v6:
time: 103 us
  Pallas kernels  102 us (99%)
    pallas_call x1, Pallas kernels, body(): pl.pallas_call(kernel, out_shape=(jax.ShapeDtypeStruct((1, ROWS), F32), j...  100 us

profile of v6, /device:TPU:1, one launch (start us, length us, event | category | flops | bytes accessed | tf_op | source)
XLA Modules:
  0.0 102.6 jit_solution(8328851182237583551)
XLA Ops:
  0.6 100.4 %align.1 = (f32[1,128]{1,0:T(1,128)}, f32[32,768]{1,0:T(8,128)}, f32[32,384]{1,0:T(8,128)}) custom-call(bf16[128,768]{1,0:T(8,128)(2,1)} %q_hbm.1, bf16[128,768]{1,0:T(8,128)(2,1)} %k_hbm.1, bf16[128,768]{1,0:T(8,128)(2,1)} %v_hbm.1, bf16[128,768]{1,0:T(8,128)(2,1)} %res_hbm.1, s32[1,4096]{1,0:T(1,128)} %seg_ref.1, s32[1,32]{1,0:T(1,128)} %cnt_ref.1, ...), custom_call_target="tpu_custom_call" | custom-call | tf_op jit(solution)/shard_map/align/pallas_call | solution.py:591
  101.0 1.6 %hand_on.1 = (f32[1,128]{1,0:T(1,128)}, f32[32,768]{1,0:T(8,128)}, f32[32,384]{1,0:T(8,128)}) custom-call(f32[1,128]{1,0:T(1,128)} %get-tuple-element.9.a, f32[32,768]{1,0:T(8,128)} %get-tuple-element.10.b, f32[32,384]{1,0:T(8,128)} %get-tuple-element.11.c), custom_call_target="tpu_custom_call" | custom-call | tf_op jit(solution)/shard_map/hand_on/pallas_call | solution.py:616

commit v7 on v6

--- a/solution.py
+++ b/solution.py
@@ -48,9 +48,9 @@
     opart, stats, oin, sin,
     esend, erecv, share, estat, estat_in, packed, arecv, aturn, alast, tsend, tgt,
     hgrp, fpart, frecv, first, act_rows, second, bsend, bgrp, alall, column_weight,
-    apiece, agrp, dpiece, dgrp, gz, gz_in, segrow,
+    apiece, agrp, dpiece, dgrp, go_z, go_in, gi_z, gi_in, segrow,
     lsem, q_s, q_r, kv_s, kv_r, o_s, o_r, os_s, os_r, x_s, x_r, pc_s, pc_r, pr_s, pr_r, ay_s, ay_r, az_s, az_r,
-    gx_s, gx_r, gy_s, gy_r, gz_s, gz_r, gg_s, gg_r,
+    gx_s, gx_r, gy_s, gy_r, gz_s, gz_r, gg_s, gg_r, gi_s, gi_r,
 ):
     sec = lax.axis_index("section")
     seq = lax.axis_index("seq")
@@ -74,7 +74,7 @@
     local = []
     for n, (src, dst) in enumerate((
         (q_hbm, qbuf.at[0]), (k_hbm, kbuf.at[0]), (v_hbm, vbuf.at[0]), (eh_hbm, ehv), (ed_hbm, edv),
-        (er_hbm, erv), (res_hbm, resv), (pin_hbm, pin), (pout_hbm, pfull.at[0]),
+        (er_hbm, erv), (res_hbm, resv), (pin_hbm, pin), (pout_hbm, pfull.at[:, pl.ds(0, CH)]),
     )):
         copy = pltpu.make_async_copy(src, dst, lsem.at[n])
         local.append(copy)
@@ -139,25 +139,17 @@
     def core_copy(n, ref):
         return rcopy(ref, ref, gx_s.at[n], gx_r.at[n], {"section": 1 - sec})
 
-    def group_copies(n, pieces, group):
+    def group_copies(n, piece_of, slot):
         copies = []
         for ds in range(2):
             for r in range(NY):
                 if ds or r:
                     to_sec, to_y = lax.rem(sec + ds, 2), lax.rem(y + r, NY)
                     copies.append(rcopy(
-                        pieces.at[to_sec, to_y], group.at[x, sec, y],
+                        piece_of(to_sec, to_y), slot,
                         gg_s.at[n, ds * NY + r], gg_r.at[n, ds * NY + (NY - r) % NY],
                         {"section": to_sec, "seq": to_y * NZ + z}))
         return copies
-
-    def send_pieces(copies, rows, pieces, group):
-        for a in range(2):
-            for b in range(NY):
-                pieces[a, b] = rows[:, (a * NY + b) * 256:(a * NY + b + 1) * 256]
-        for copy in copies:
-            go(copy)
-        group[x, sec, y] = pieces[sec, y]
 
     local[3].wait()
     local[4].wait()
@@ -169,15 +161,18 @@
             go(enc_copies[r])
 
     core_rows = pl.ds(pl.multiple_of(sec * (PROJ // 2), PROJ // 2), PROJ // 2)
-    p_copies = x_copies(9, lambda r: pfull.at[0, core_rows], lambda r: pfull.at[r, core_rows], (1, 3))
+    def out_block(rows, r):
+        return pfull.at[rows, pl.ds(r * CH, CH)]
+
+    p_copies = x_copies(9, lambda r: out_block(core_rows, 0), lambda r: out_block(core_rows, r), (1, 3))
 
     def relay(n):
         part = pl.ds(pl.multiple_of(sec * (PROJ // 2) + n * PART, PART), PART)
-        return rcopy(pfull.at[(3, 1)[n], part], pfull.at[2, part], pr_s.at[n], pr_r.at[n],
+        return rcopy(out_block(part, (3, 1)[n]), out_block(part, 2), pr_s.at[n], pr_r.at[n],
                      {"mp": lax.rem(x + (1, 3)[n], NX)})
 
     relays = [relay(0), relay(1)]
-    pc_copies = {r: rcopy(pfull.at[r, core_rows], pfull.at[r, core_rows], pc_s.at[r - 1], pc_r.at[r - 1],
+    pc_copies = {r: rcopy(out_block(core_rows, r), out_block(core_rows, r), pc_s.at[r - 1], pc_r.at[r - 1],
                           {"section": 1 - sec}) for r in (1, 2, 3)}
     ids = iota((16, NSEQ * ROWS), 0)
     seg = seg_ref[...]
@@ -404,9 +399,6 @@
         attn = attn.T.astype(BF16).astype(F32)
         hgrp[sec, y, :, cols] = (resv[:, cols].astype(F32) + attn).astype(BF16)
 
-    h_copies = y_copies(0, lambda: hgrp.at[sec, y])
-    for r in (2, 1, 3):
-        go(h_copies[r])
     local[7].wait()
     hidden = hgrp[sec, y]
     f_copies = []
@@ -438,8 +430,16 @@
         first[:, cols] = value
         act_rows[:, cols] = (value * jax.nn.sigmoid(value)).astype(BF16)
     act = act_rows[...]
-    act_pieces = group_copies(0, apiece, agrp)
-    send_pieces(act_pieces, act, apiece, agrp)
+    act_pieces = group_copies(0, lambda a, b: apiece.at[a, b], agrp.at[x, sec, y])
+    for a in range(2):
+        for b in range(NY):
+            apiece[a, b] = act[:, (a * NY + b) * 256:(a * NY + b + 1) * 256]
+    for copy in act_pieces:
+        go(copy)
+    agrp[x, sec, y] = apiece[sec, y]
+    h_copies = y_copies(0, lambda: hgrp.at[sec, y])
+    for r in (2, 1, 3):
+        go(h_copies[r])
     for r in range(1, NZ):
         take(row_zs[NZ - r])
     tsend[...] = dot(chosen, alast[...].reshape(CAP, CH)).astype(BF16).reshape(NX, 32, CH)
@@ -448,23 +448,25 @@
         go(t_copies[r])
     tgt[0] = tsend[x]
     column_weight[...] = jnp.broadcast_to(aw_ref[...], (ROWS, ROWS)).T
-    for r in range(NX):
-        if r:
-            take(pc_copies[r])
-        if r == 2:
-            for copy in act_pieces:
-                take(copy)
-            act_copies = x_copies(4, lambda r: agrp.at[x], lambda r: agrp.at[x])
-            for r2 in (2, 1, 3):
-                go(act_copies[r2])
-        second[r] = dot(act, pfull[r])
+    take(pc_copies[1])
+    wide = 2 * CH
+    second[:, 0:wide] = dot(act, pfull[:, 0:wide])
+    for copy in act_pieces:
+        take(copy)
+    act_copies = x_copies(4, lambda r: agrp.at[x], lambda r: agrp.at[x])
+    for r in (2, 1, 3):
+        go(act_copies[r])
+    take(pc_copies[3])
+    take(pc_copies[2])
+    second[:, wide:ENC_D] = dot(act, pfull[:, wide:ENC_D])
     for r in (1, 2, 3):
         take(t_copies[NX - r])
     inner = square_z = square_f = 0.0
     for r in range(NX):
         tf = tgt[r].astype(F32)
-        inner = inner + jnp.sum(second[r] * tf, axis=1, keepdims=True)
-        square_z = square_z + jnp.sum(second[r] * second[r], axis=1, keepdims=True)
+        value = second[:, r * CH:(r + 1) * CH]
+        inner = inner + jnp.sum(value * tf, axis=1, keepdims=True)
+        square_z = square_z + jnp.sum(value * value, axis=1, keepdims=True)
         square_f = square_f + jnp.sum(tf * tf, axis=1, keepdims=True)
     norm_z = jnp.sqrt(square_z + 1e-6)
     norm_f = jnp.sqrt(square_f + 1e-6)
@@ -474,7 +476,7 @@
     by_second = weight * aligned / (norm_z * norm_z)
     b_copies = x_copies(6, lambda r: bsend.at[r], lambda r: bgrp.at[sec, y, x])
     for r in (2, 1, 3, 0):
-        bsend[r] = (by_target * tgt[r].astype(F32) + by_second * second[r]).astype(BF16)
+        bsend[r] = (by_target * tgt[r].astype(F32) + by_second * second[:, r * CH:(r + 1) * CH]).astype(BF16)
         if r:
             go(b_copies[r])
     bgrp[sec, y, x] = bsend[0]
@@ -482,14 +484,30 @@
     l_copies = x_copies(7, lambda r: alall.at[x], lambda r: alall.at[x])
     for r in (2, 1, 3):
         go(l_copies[r])
-    upstream = dot(bsend[0], pfull[0], 1, 1)
-    for r in (1, 2, 3):
-        upstream = upstream + dot(bsend[r], pfull[r], 1, 1)
+    upstream = dot(jnp.concatenate([bsend[r] for r in range(NX)], axis=1), pfull[...], 1, 1)
     value = first[...]
     sig = jax.nn.sigmoid(value)
     dfirst = (upstream * sig * (1.0 + value * (1.0 - sig))).astype(BF16)
-    d_pieces = group_copies(1, dpiece, dgrp)
-    send_pieces(d_pieces, dfirst, dpiece, dgrp)
+    d_pieces = group_copies(1, lambda a, b: dpiece.at[:, a, b], dgrp.at[:, x, sec, y])
+    place = iota((CAP, CAP), 1)
+    origin = ((2 * ((place >> 5) & 3) + (place >> 7)) << 5) + (place & 31)
+    order = jnp.where(iota((CAP, CAP), 0) == origin, 1.0, 0.0).astype(BF16)
+    for a in range(2):
+        for b in range(NY):
+            columns = dot(dfirst[:, (a * NY + b) * CAP:(a * NY + b + 1) * CAP], order).astype(BF16)
+            for half in range(2):
+                dpiece[half, a, b] = columns[:, half * HD:(half + 1) * HD]
+    for copy in d_pieces:
+        go(copy)
+    for half in range(2):
+        dgrp[half, x, sec, y] = dpiece[half, sec, y]
+    for copy in d_pieces:
+        take(copy)
+    d_copies = []
+    for half in range(2):
+        d_copies.append(x_copies(8 + 2 * half, lambda r: dgrp.at[half, x], lambda r: dgrp.at[half, x]))
+        for r in (2, 1, 3):
+            go(d_copies[half][r])
     for r in (1, 2, 3):
         take(b_copies[NX - r])
     back_copies = y_copies(1, lambda: bgrp.at[sec, y])
@@ -499,11 +517,6 @@
         take(h_copies[NY - r])
     hidden_core = core_copy(0, hgrp.at[sec])
     go(hidden_core)
-    for copy in d_pieces:
-        take(copy)
-    d_copies = x_copies(8, lambda r: dgrp.at[x], lambda r: dgrp.at[x])
-    for r in (2, 1, 3):
-        go(d_copies[r])
     for r in (1, 2, 3):
         take(l_copies[NX - r])
     al_ref[...] = alall[...].reshape(ROWS, HD).T[0:1]
@@ -515,42 +528,53 @@
         take(act_copies[NX - r])
     take(back_core)
 
-    def z_copies(n):
-        copies = {}
-        for r in range(1, NZ):
-            peer = lax.rem(z + r, NZ)
-            copies[r] = rcopy(gz.at[n, peer], gz_in.at[n, NZ - r], gz_s.at[n, r - 1], gz_r.at[n, NZ - r - 1],
-                              {"seq": y * NZ + peer})
-        return copies
-
-    z_all = [z_copies(n) for n in range(3)]
-
-    def product(n, left, right_of):
+    def go_copy(r):
+        peer = lax.rem(z + r, NZ)
+        return rcopy(go_z.at[peer], go_in.at[NZ - r], gz_s.at[r - 1], gz_r.at[NZ - r - 1], {"seq": y * NZ + peer})
+
+    go_copies = {r: go_copy(r) for r in range(1, NZ)}
+    value = 0.0
+    for b in range(NX):
+        value = value + dot(agrp[b].reshape(CAP, CAP), bgrp[:, :, b].reshape(CAP, CH), 0, 0)
+    go_z[...] = value.astype(BF16).reshape(NZ, 32, CH)
+    for r in (4, 3, 5, 2, 6, 1, 7):
+        go(go_copies[r])
+    take(hidden_core)
+
+    def gi_copy(peer, mine):
+        return rcopy(gi_z.at[lax.rem(peer, 2), peer // 2], gi_in.at[mine], gi_s.at[peer], gi_r.at[mine],
+                     {"seq": y * NZ + peer})
+
+    for half in range(2):
+        for r in (1, 2, 3):
+            take(d_copies[half][NX - r])
         value = 0.0
         for b in range(NX):
-            rows = left[b].reshape(CAP, CAP)
-            value = value + dot(rows, right_of(b).reshape(CAP, CH), 0, 0)
-        gz[n] = value.astype(BF16).reshape(NZ, 32, CH)
-        for r in (4, 3, 5, 2, 6, 1, 7):
-            go(z_all[n][r])
-
-    def finish(n):
-        for r in range(1, NZ):
-            take(z_all[n][NZ - r])
-        value = gz[n, z].astype(F32)
-        for r in range(1, NZ):
-            value = value + gz_in[n, r].astype(F32)
-        return value
-
-    product(0, agrp, lambda b: bgrp[:, :, b])
-    take(hidden_core)
-    for r in (1, 2, 3):
-        take(d_copies[NX - r])
-    for n in range(2):
-        product(1 + n, dgrp, lambda b: hgrp[:, :, b * 32:(b + 1) * 32, n * CH:(n + 1) * CH])
-    go_ref[...] = finish(0)
-    for n in range(2):
-        gi_ref[:, n * CH:(n + 1) * CH] = finish(1 + n)
+            rows = hgrp[:, :, b * 32:(b + 1) * 32].reshape(CAP, WIDTH)
+            value = value + dot(dgrp[half, b].reshape(CAP, HD), rows, 0, 0)
+        gi_z[half] = value.astype(BF16).reshape(4, 32, WIDTH)
+        odd = lax.rem(z + half, 2)
+        for m in (2, 1, 3):
+            gi_copy(lax.rem(z + odd + 2 * m, NZ), z).start()
+
+        @pl.when(odd == 1)
+        def _():
+            gi_copy(lax.rem(z + 1, NZ), z).start()
+
+    for r in range(1, NZ):
+        take(go_copies[NZ - r])
+    value = go_z[z].astype(F32)
+    for r in range(1, NZ):
+        value = value + go_in[r].astype(F32)
+    go_ref[...] = value
+    value = gi_z[lax.rem(z, 2), z // 2].astype(F32)
+    for r in range(1, NZ):
+        peer = lax.rem(z + r, NZ)
+        gi_copy(z, peer).wait_recv()
+        value = value + gi_in[peer].astype(F32)
+    gi_ref[...] = value
+    for r in range(1, NZ):
+        gi_copy(lax.rem(z + r, NZ), z).wait_send()
 
     for copy in pending:
         copy.wait_send()
@@ -567,7 +591,7 @@
         V((NZ, ROWS, WIDTH), BF16), V((NY, ROWS, WIDTH), BF16), V((NY, ROWS, WIDTH), BF16),
         V((WIDTH, NY * ROWS), BF16), V((NY, ROWS, HD), BF16), V((ROWS, WIDTH), BF16),
         V((CAP, FF), BF16), V((FF, ENC_D), BF16), V((CAP, CH), BF16),
-        V((WIDTH, PROJ), BF16), V((NX, PROJ, CH), BF16),
+        V((WIDTH, PROJ), BF16), V((PROJ, ENC_D), BF16),
         V((NZ, 2, HALF, HD), BF16), V((NZ, 2, 8, HD), F32),
         V((2, 4, 2, HALF, HD), BF16), V((2, 4, 2, 8, HD), F32),
         V((NX, CAP, CH), BF16), V((NX, CAP, CH), BF16), V((CAP, CH), F32),
@@ -575,18 +599,18 @@
         V((NY, NZ, 8, CH), F32), V((NY, NZ, 8, CH), F32), V((NZ, 32, CH), BF16), V((NZ, 32, CH), BF16),
         V((NX, 32, CH), BF16), V((NX, 32, CH), BF16),
         V((2, NY, ROWS, WIDTH), BF16), V((NX, 32, PROJ), BF16), V((NX, 32, PROJ), BF16), V((32, PROJ), F32),
-        V((32, PROJ), BF16), V((NX, 32, CH), F32), V((NX, 32, CH), BF16), V((2, NY, NX, 32, CH), BF16),
+        V((32, PROJ), BF16), V((32, ENC_D), F32), V((NX, 32, CH), BF16), V((2, NY, NX, 32, CH), BF16),
         V((NX, 32, HD), F32), V((ROWS, ROWS), F32),
         V((2, NY, 32, 256), BF16), V((NX, 2, NY, 32, 256), BF16),
-        V((2, NY, 32, 256), BF16), V((NX, 2, NY, 32, 256), BF16),
-        V((3, NZ, 32, CH), BF16), V((3, NZ, 32, CH), BF16),
+        V((2, 2, NY, 32, HD), BF16), V((2, NX, 2, NY, 32, HD), BF16),
+        V((NZ, 32, CH), BF16), V((NZ, 32, CH), BF16), V((2, 4, 32, WIDTH), BF16), V((NZ, 32, WIDTH), BF16),
         V((2, HD, HD), F32),
     ]
     scratch += [
         D((9,)), D((2, 4, 2)), D((2, 4, 2)), D((6,)), D((6,)),
         D((2, 4, 2)), D((2, 4, 2)), D((2, 4, 2)), D((2, 4, 2)),
-        D((10, 3)), D((10, 3)), D((3,)), D((3,)), D((2,)), D((2,)), D((3,)), D((3,)), D((7,)), D((7,)),
-        D((2,)), D((2,)), D((2, 3)), D((2, 3)), D((3, 7)), D((3, 7)), D((2, 8)), D((2, 8)),
+        D((11, 3)), D((11, 3)), D((3,)), D((3,)), D((2,)), D((2,)), D((3,)), D((3,)), D((7,)), D((7,)),
+        D((2,)), D((2,)), D((2, 3)), D((2, 3)), D((7,)), D((7,)), D((2, 8)), D((2, 8)), D((8,)), D((8,)),
     ]
     aligned, grad_in_t, grad_out = pl.pallas_call(
         kernel,

time: 103 us -> 103 us (level)
  no operation moved by 1% of the time
where the time goes in v7:
time: 103 us
  Pallas kernels  102 us (99%)
    pallas_call x1, Pallas kernels, body(): pl.pallas_call(kernel, out_shape=(jax.ShapeDtypeStruct((1, ROWS), F32), j...  101 us

profile of v7, /device:TPU:1, one launch (start us, length us, event | category | flops | bytes accessed | tf_op | source)
XLA Modules:
  0.0 102.8 jit_solution(607410441893605484)
XLA Ops:
  0.6 100.6 %align.1 = (f32[1,128]{1,0:T(1,128)}, f32[32,768]{1,0:T(8,128)}, f32[32,384]{1,0:T(8,128)}) custom-call(bf16[128,768]{1,0:T(8,128)(2,1)} %q_hbm.1, bf16[128,768]{1,0:T(8,128)(2,1)} %k_hbm.1, bf16[128,768]{1,0:T(8,128)(2,1)} %v_hbm.1, bf16[128,768]{1,0:T(8,128)(2,1)} %res_hbm.1, s32[1,4096]{1,0:T(1,128)} %seg_ref.1, s32[1,32]{1,0:T(1,128)} %cnt_ref.1, ...), custom_call_target="tpu_custom_call" | custom-call | tf_op jit(solution)/shard_map/align/pallas_call | solution.py:615
  101.3 1.6 %hand_on.1 = (f32[1,128]{1,0:T(1,128)}, f32[32,768]{1,0:T(8,128)}, f32[32,384]{1,0:T(8,128)}) custom-call(f32[1,128]{1,0:T(1,128)} %get-tuple-element.9.a, f32[32,768]{1,0:T(8,128)} %get-tuple-element.10.b, f32[32,384]{1,0:T(8,128)} %get-tuple-element.11.c), custom_call_target="tpu_custom_call" | custom-call | tf_op jit(solution)/shard_map/hand_on/pallas_call | solution.py:640

commit v8 on v7

--- a/solution.py
+++ b/solution.py
@@ -113,7 +113,7 @@
     kv_copies = [kv_copy(n) for n in range(6)]
     for n in range(3):
         local[n].wait()
-    fetch(3, 9)
+    fetch(3, 5)
     for half in range(2):
         for d in range(2):
             go(q_copies[d][0][half])
@@ -160,6 +160,7 @@
         if r:
             go(enc_copies[r])
 
+    fetch(5, 9)
     core_rows = pl.ds(pl.multiple_of(sec * (PROJ // 2), PROJ // 2), PROJ // 2)
     def out_block(rows, r):
         return pfull.at[rows, pl.ds(r * CH, CH)]
@@ -334,9 +335,9 @@
     take(kv_copies[2])
     for r in (0, 1, 3):
         turn_values(r)
-    forward_q(2, 0)
     sum_encoder()
     gather_out()
+    forward_q(2, 0)
     forward_q(2, 1)
     for n in (4, 5):
         take(kv_copies[n])
@@ -375,7 +376,7 @@
                 take_o(d, t - 1, half)
                 merge(4 - t if d == 0 else 4 + t, d, t - 1, half)
                 go_o(d, t, half)
-        if t == 2:
+        if t == 1:
             relay_out()
     for r in (1, 2, 3):
         take(row_ys[NY - r])
@@ -388,9 +389,6 @@
         for d in range(2):
             take_o(d, 3, half)
             merge(0, d, 3, half)
-    for n in range(2):
-        take(relays[n])
-    go(pc_copies[2])
     local[6].wait()
     for h in range(HEADS):
         half, i = h // 3, h % 3
@@ -409,6 +407,9 @@
             2 + c, lambda r: fpart.at[lax.rem(x + r, NX), :, cols], lambda r: frecv.at[r, :, cols]))
         for r in (2, 1, 3):
             go(f_copies[c][r])
+    for n in range(2):
+        take(relays[n])
+    go(pc_copies[2])
     column = iota((NSEQ, CAP), 1)
     e_of = ((column >> 3) & (NY - 1)) * NZ + (column >> 5)
     device = iota((NSEQ, CAP), 0)

time: 103 us -> 106 us (1.029)
  Pallas kernels: 102 us -> 105 us
    pallas_call x1, Pallas kernels: 101 us -> 104 us  [body(): pl.pallas_call(kernel, out_shape=(jax.ShapeDtypeStruct((1, ROWS), F32), j...]
where the time goes in v8:
time: 106 us
  Pallas kernels  105 us (99%)
    pallas_call x1, Pallas kernels, body(): pl.pallas_call(kernel, out_shape=(jax.ShapeDtypeStruct((1, ROWS), F32), j...  104 us

profile of v8, /device:TPU:1, one launch (start us, length us, event | category | flops | bytes accessed | tf_op | source)
XLA Modules:
  0.0 105.9 jit_solution(1563610823244583234)
XLA Ops:
  0.6 103.7 %align.1 = (f32[1,128]{1,0:T(1,128)}, f32[32,768]{1,0:T(8,128)}, f32[32,384]{1,0:T(8,128)}) custom-call(bf16[128,768]{1,0:T(8,128)(2,1)} %q_hbm.1, bf16[128,768]{1,0:T(8,128)(2,1)} %k_hbm.1, bf16[128,768]{1,0:T(8,128)(2,1)} %v_hbm.1, bf16[128,768]{1,0:T(8,128)(2,1)} %res_hbm.1, s32[1,4096]{1,0:T(1,128)} %seg_ref.1, s32[1,32]{1,0:T(1,128)} %cnt_ref.1, ...), custom_call_target="tpu_custom_call" | custom-call | tf_op jit(solution)/shard_map/align/pallas_call | solution.py:616
  104.4 1.6 %hand_on.1 = (f32[1,128]{1,0:T(1,128)}, f32[32,768]{1,0:T(8,128)}, f32[32,384]{1,0:T(8,128)}) custom-call(f32[1,128]{1,0:T(1,128)} %get-tuple-element.9.a, f32[32,768]{1,0:T(8,128)} %get-tuple-element.10.b, f32[32,384]{1,0:T(8,128)} %get-tuple-element.11.c), custom_call_target="tpu_custom_call" | custom-call | tf_op jit(solution)/shard_map/hand_on/pallas_call | solution.py:641

commit v9 on v8

--- a/solution.py
+++ b/solution.py
@@ -335,9 +335,9 @@
     take(kv_copies[2])
     for r in (0, 1, 3):
         turn_values(r)
+    forward_q(2, 0)
     sum_encoder()
     gather_out()
-    forward_q(2, 0)
     forward_q(2, 1)
     for n in (4, 5):
         take(kv_copies[n])
@@ -376,7 +376,7 @@
                 take_o(d, t - 1, half)
                 merge(4 - t if d == 0 else 4 + t, d, t - 1, half)
                 go_o(d, t, half)
-        if t == 1:
+        if t == 3:
             relay_out()
     for r in (1, 2, 3):
         take(row_ys[NY - r])

time: 106 us -> 101 us (0.953)
  Pallas kernels: 105 us -> 100 us
    pallas_call x1, Pallas kernels: 104 us -> 98.6 us  [body(): pl.pallas_call(kernel, out_shape=(jax.ShapeDtypeStruct((1, ROWS), F32), j...]
where the time goes in v9:
time: 101 us
  Pallas kernels  100 us (99%)
    pallas_call x1, Pallas kernels, body(): pl.pallas_call(kernel, out_shape=(jax.ShapeDtypeStruct((1, ROWS), F32), j...  98.6 us

profile of v9, /device:TPU:1, one launch (start us, length us, event | category | flops | bytes accessed | tf_op | source)
XLA Modules:
  0.0 100.8 jit_solution(9655038194356873264)
XLA Ops:
  0.6 98.6 %align.1 = (f32[1,128]{1,0:T(1,128)}, f32[32,768]{1,0:T(8,128)}, f32[32,384]{1,0:T(8,128)}) custom-call(bf16[128,768]{1,0:T(8,128)(2,1)} %q_hbm.1, bf16[128,768]{1,0:T(8,128)(2,1)} %k_hbm.1, bf16[128,768]{1,0:T(8,128)(2,1)} %v_hbm.1, bf16[128,768]{1,0:T(8,128)(2,1)} %res_hbm.1, s32[1,4096]{1,0:T(1,128)} %seg_ref.1, s32[1,32]{1,0:T(1,128)} %cnt_ref.1, ...), custom_call_target="tpu_custom_call" | custom-call | tf_op jit(solution)/shard_map/align/pallas_call | solution.py:616
  99.2 1.6 %hand_on.1 = (f32[1,128]{1,0:T(1,128)}, f32[32,768]{1,0:T(8,128)}, f32[32,384]{1,0:T(8,128)}) custom-call(f32[1,128]{1,0:T(1,128)} %get-tuple-element.9.a, f32[32,768]{1,0:T(8,128)} %get-tuple-element.10.b, f32[32,384]{1,0:T(8,128)} %get-tuple-element.11.c), custom_call_target="tpu_custom_call" | custom-call | tf_op jit(solution)/shard_map/hand_on/pallas_call | solution.py:641
